TPU v7x, 32 devices: a whole 2x2x4 slice. The times are simulated.
32 devices in a mesh: req: 8 (over z, y), tp: 4 (over x, core).
Axes of the slice: x: 2, y: 2, z: 4, core: 2. Of those that a mesh axis runs over, the one named last changes fastest.
Arguments:
- hidden: bfloat16 [8192, 2560], P('req'), may hold values from -6 to 6
- segments: int32 [8, 1024], P('req'), may hold values from 0 to 7, never falling along the last dimension, each value on 1 to 512 neighbouring positions
- send_order: int32 [8, 1024], P('req'), may hold values from 0 to 1023, each once within a row
- page_table: int32 [8, 64], replicated, may hold values from 0 to 511, as said below
- norm_gain: bfloat16 [2560], replicated, may hold values from 0.5 to 1.5
- w_query: bfloat16 [2560, 2560], P(None, 'tp'), may hold values from -0.125 to 0.125
- w_key: bfloat16 [2560, 640], P(None, 'tp'), may hold values from -0.125 to 0.125
- w_value: bfloat16 [2560, 640], P(None, 'tp'), may hold values from -0.125 to 0.125
- w_output: bfloat16 [2560, 2560], P('tp'), may hold values from -0.125 to 0.125
Outputs:
- hidden_out: bfloat16 [8192, 2560], P('req', 'tp')
- kv_cache: bfloat16 [512, 16, 8, 160], P('req', None, 'tp')
Inputs may be any that keep to these rules, and one draw needn't show every extreme that they name: `send_order`: each row lists every local token once; the token in send position j goes to the device of req index j // 128. `segments`: never falling along a block; a prompt lies within one block. `page_table`: every cache page appears once in the whole table; page q belongs to req index q // 64, and each row names exactly 8 pages of each req index.
All inputs are finite; a program needn't handle non-finite values.
Results may differ from a plain program's by a relative error of at most 0.006.
Values may be sent and summed in bfloat16 or wider, within the bound.
A program may use at most 128 MiB of HBM per device.

v0:
```python
import functools
import math

import jax
import jax.numpy as jnp
from jax import lax
from jax.experimental import pallas as pl
from jax.experimental.pallas import tpu as pltpu
from jax.sharding import PartitionSpec as P

HD = 80
PAGE = 16
LONGEST = 512

eps_norm = 1e-05
rope_base = 1000000.0
F32 = jnp.float32
BF16 = jnp.bfloat16


LANES = 128


def padded_halves(array):
    rows = array.shape[0]
    split = array.reshape(rows, -1, 2, HD // 2)
    return jnp.pad(split, ((0, 0), (0, 0), (0, 0), (0, (LANES - HD) // 2))).reshape(rows, -1)


def padded_heads(array, axis):
    shape = array.shape
    split = array.reshape(shape[:axis] + (-1, HD) + shape[axis + 1 :])
    widths = [(0, 0)] * split.ndim
    widths[axis + 1] = (0, LANES - HD)
    return jnp.pad(split, widths).reshape(shape[:axis] + (-1,) + shape[axis + 1 :])


def rope_tables(segment_row):
    length = segment_row.shape[0]
    places = jnp.arange(length, dtype=jnp.int32)
    first_index = jnp.sum((segment_row[None, :] < segment_row[:, None]).astype(jnp.int32), axis=1)
    position = (places - first_index).astype(F32)
    frequency = rope_base ** (-jnp.arange(0, HD, 2, dtype=F32) / HD)
    angles = position[:, None] * frequency[None, :]
    cosine, sine = jnp.cos(angles), jnp.sin(angles)
    cosine = padded_halves(jnp.concatenate([cosine, cosine], axis=-1))
    sine = padded_halves(jnp.concatenate([-sine, sine], axis=-1))
    return cosine, sine, first_index


def attention_kernel(cuts, groups, heads, kv, steps, *refs):
    raw_refs, refs = refs[: len(cuts)], refs[len(cuts) :]
    cos_ref, sin_ref, first_ref = refs[:3]
    out_refs, refs = refs[3 : 3 + steps], refs[3 + steps :]
    key_ref, value_ref, query_scr, value_scr = refs
    share = cuts[-1][1]
    length = groups * share
    scale = math.log2(math.e) / math.sqrt(HD)

    for (low, high), raw_ref in zip(cuts, raw_refs):
        size = high - low

        @pl.loop(0, groups)
        def _(g):
            here = pl.ds(pl.multiple_of(g * size, 16), size)
            there = pl.ds(pl.multiple_of(g * share + low, 16), size)
            cosine, sine = cos_ref[there, :], sin_ref[there, :]
            for h in range(heads + kv):
                x = raw_ref[here, h * LANES : (h + 1) * LANES]
                turned = x * cosine + pltpu.roll(x, LANES // 2, 1) * sine
                if h < heads:
                    query_scr[there, h * LANES : (h + 1) * LANES] = turned.astype(BF16)
                else:
                    at = (h - heads) * LANES
                    key_ref[there, at : at + LANES] = turned.astype(BF16)
            lane = lax.broadcasted_iota(jnp.int32, (size, LANES), 1)
            for h in range(kv):
                at = (heads + kv + h) * LANES
                x = raw_ref[here, at : at + LANES]
                value_ref[there, h * LANES : (h + 1) * LANES] = x.astype(BF16)
                value_scr[there, h * LANES : (h + 1) * LANES] = jnp.where(
                    lane == HD, 1.0, x
                ).astype(BF16)

    tile = 256 if length % 256 == 0 else length
    ratio = heads // kv
    for low in range(0, length, tile):
        high = low + tile
        start = max(0, low - LONGEST)
        keys = high - start
        key_place = start + lax.broadcasted_iota(jnp.int32, (tile, keys), 1)
        query_place = low + lax.broadcasted_iota(jnp.int32, (tile, keys), 0)
        allowed = (key_place >= first_ref[low:high, :]) & (key_place <= query_place)

        @pl.loop(0, heads)
        def _(h):
            mine = pl.ds(pl.multiple_of(h * LANES, LANES), LANES)
            shared = pl.ds(pl.multiple_of((h // ratio) * LANES, LANES), LANES)
            scores = lax.dot_general(
                query_scr[low:high, mine], key_ref[start:high, shared],
                (((1,), (1,)), ((), ())), preferred_element_type=F32,
            )
            probs = jnp.where(allowed, jnp.exp2(scores * scale), 0.0).astype(BF16)
            sums = jnp.dot(probs, value_scr[start:high, shared], preferred_element_type=F32)
            done = (sums / sums[:, HD : HD + 1]).astype(BF16)
            run = share // steps
            for block in range(tile // run):
                g, step = divmod(low // run + block, steps)
                out_refs[step][g * run : (g + 1) * run, mine] = done[block * run : (block + 1) * run]


def attention(raw_parts, cuts, groups, heads, kv, steps, tables):
    cosine, sine, first_index = tables
    length = groups * cuts[-1][1]
    shapes = [jax.ShapeDtypeStruct((length // steps, heads * LANES), BF16)] * steps
    shapes += [jax.ShapeDtypeStruct((length, kv * LANES), BF16)] * 2
    whole = pl.BlockSpec(memory_space=pltpu.VMEM)
    outs = pl.pallas_call(
        functools.partial(attention_kernel, cuts, groups, heads, kv, steps),
        out_shape=shapes,
        in_specs=[whole] * (len(cuts) + 3),
        out_specs=[whole] * len(shapes),
        scratch_shapes=[
            pltpu.VMEM((length, heads * LANES), BF16),
            pltpu.VMEM((length, kv * LANES), BF16),
        ],
        compiler_params=pltpu.CompilerParams(vmem_limit_bytes=40 * 2**20),
        cost_estimate=pl.CostEstimate(
            flops=4 * length * 640 * heads * LANES, bytes_accessed=10 * 2**20,
            transcendentals=length * 640 * heads,
        ),
    )(*raw_parts, cosine, sine, first_index[:, None])
    return outs[:steps], outs[steps], outs[steps + 1]


def one_hot_rows(index, count):
    return (index[:, None] == jnp.arange(count, dtype=jnp.int32)[None, :]).astype(BF16)


def local(hidden, segments, send_order, page_table, norm_gain, w_query, w_key, w_value, w_output):
    groups = lax.axis_size("req")
    tp_count = lax.axis_size("tp")
    length, width = hidden.shape
    share = length // groups
    part = width // tp_count
    cores = 2 if tp_count % 2 == 0 else 1
    xs = tp_count // cores
    tp_place = lax.axis_index("tp")
    my_x, my_core = tp_place // cores, tp_place % cores
    order_grid = send_order[0].reshape(groups, share)
    segment_row = segments[0]

    def piece(k, e):
        return lax.rem(my_x + k, xs) * cores + (my_core ^ e)

    def from_x(array, k):
        pairs = [
            (((x + k) % xs) * cores + c, x * cores + c) for x in range(xs) for c in range(cores)
        ]
        return lax.ppermute(array, "tp", pairs)

    def from_core(array):
        pairs = [(x * cores + (c ^ 1), x * cores + c) for x in range(xs) for c in range(cores)]
        return lax.ppermute(array, "tp", pairs)

    own_core = [piece(k, 0) for k in range(xs)]
    all_pieces = own_core + ([piece(k, 1) for k in range(xs)] if cores == 2 else [])

    widened = hidden.astype(F32)
    inverse_rms = lax.rsqrt(jnp.mean(widened * widened, axis=-1, keepdims=True) + eps_norm)

    def normed_columns(p):
        columns = lax.dynamic_slice_in_dim(hidden, p * part, part, 1).astype(F32)
        gain = lax.dynamic_slice_in_dim(norm_gain, p * part, part, 0).astype(F32)
        return (columns * inverse_rms * gain).astype(BF16)

    normed_own = [normed_columns(p) for p in own_core]

    cut = max(1, (share * 5 // 8) // 16) * 16 if share > 16 else share
    cuts = [(0, cut), (cut, share)] if cut < share else [(0, share)]

    def deal(columns, low, high):
        sent = jnp.dot(
            one_hot_rows(order_grid[:, low:high].reshape(-1), length), columns,
            preferred_element_type=F32,
        ).astype(BF16)
        return lax.all_to_all(sent, "req", split_axis=0, concat_axis=0, tiled=True)

    weights = jnp.concatenate(
        [padded_halves(w_query), padded_halves(w_key), padded_heads(w_value, 1)], axis=1
    )
    weights = jnp.concatenate(
        [lax.dynamic_slice_in_dim(weights, p * part, part, 0) for p in all_pieces], axis=0
    )
    out_weights = [lax.dynamic_slice_in_dim(w_output, p * part, part, 1) for p in all_pieces]
    out_keep = padded_heads(jnp.concatenate(out_weights[:xs], axis=1), 0)
    out_send = padded_heads(jnp.concatenate(out_weights[xs:], axis=1), 0) if cores == 2 else None

    raw_parts = []
    for number, (low, high) in enumerate(cuts):
        if number == 0:
            mine = deal(normed_own[0], low, high)
            mine = jnp.concatenate([mine] + [from_x(mine, k) for k in range(1, xs)], axis=1)
        else:
            mine = deal(jnp.concatenate(normed_own, axis=1), low, high)
        half = mine.shape[1]
        raw = jnp.dot(mine, weights[:half], preferred_element_type=F32)
        if cores == 2:
            other = from_core(mine)
            raw = raw + jnp.dot(other, weights[half:], preferred_element_type=F32)
        raw_parts.append(raw)

    heads_local, kv_local = w_query.shape[1] // HD, w_key.shape[1] // HD
    steps = 2 if share % 32 == 0 else 1
    attended, key_pad, value_pad = attention(
        raw_parts, cuts, groups, heads_local, kv_local, steps, rope_tables(segment_row)
    )

    total = lax.dynamic_slice_in_dim(hidden, tp_place * part, part, 1).astype(F32)
    kept_parts = []
    came_parts = [None] * steps
    if cores == 2:
        came_parts = [
            from_core(jnp.dot(rows, out_send, preferred_element_type=F32).astype(BF16))
            for rows in attended
        ]
    for rows, came in zip(attended, came_parts):
        kept = jnp.dot(rows, out_keep, preferred_element_type=F32)
        kept_parts.append(kept if came is None else kept + came.astype(F32))
    leaving_parts = [
        [kept[:, k * part : (k + 1) * part].astype(BF16) for k in range(1, xs)]
        for kept in kept_parts
    ]
    kept_parts = [kept[:, :part] for kept in kept_parts]
    kept_parts, leaving_parts = lax.optimization_barrier((kept_parts, leaving_parts))
    for step in range(steps):
        low, high = step * share // steps, (step + 1) * share // steps
        summed = kept_parts[step]
        for k in range(1, xs):
            summed = summed + from_x(leaving_parts[step][k - 1], xs - k).astype(F32)
        returned = lax.all_to_all(
            summed.astype(BF16), "req", split_axis=0, concat_axis=0, tiled=True
        )
        back = one_hot_rows(order_grid[:, low:high].reshape(-1), length)
        total = total + lax.dot_general(
            back, returned, (((0,), (0,)), ((), ())), preferred_element_type=F32
        )
    hidden_out = total.astype(BF16)

    pages_dev = length // PAGE
    per_owner = pages_dev // groups
    my_req = lax.axis_index("req")
    owners = page_table // pages_dev
    numbers = jnp.arange(pages_dev, dtype=jnp.int32)
    earlier = (owners[:, None, :] == owners[:, :, None]) & (numbers[None, :] < numbers[:, None])
    rank = jnp.sum(earlier.astype(jnp.int32), axis=-1)
    my_slots = lax.dynamic_slice_in_dim(owners * per_owner + rank, my_req, 1, 0)[0]
    half = HD // 2
    columns = []
    for h in range(kv_local):
        at = h * LANES
        columns += [
            key_pad[:, at : at + half],
            key_pad[:, at + LANES // 2 : at + LANES // 2 + half],
            value_pad[:, at : at + HD],
        ]
    kv_rows = jnp.concatenate(columns, axis=1)
    page_rows = kv_rows.reshape(pages_dev, PAGE * kv_local * 2 * HD)
    page_rows = jnp.dot(
        (my_slots[None, :] == numbers[:, None]).astype(BF16), page_rows,
        preferred_element_type=F32,
    ).astype(BF16)
    arrived = lax.all_to_all(page_rows, "req", split_axis=0, concat_axis=0, tiled=True)
    slot_here = jnp.where(
        owners == my_req, jnp.arange(groups, dtype=jnp.int32)[:, None] * per_owner + rank, -1
    ).reshape(-1)
    target = (page_table % pages_dev).reshape(-1)
    hit = (slot_here[:, None] == numbers[None, :]).astype(jnp.int32)
    slot_target = jnp.sum(hit * target[:, None], axis=0)
    place = (slot_target[None, :] == numbers[:, None]).astype(BF16)
    kv_cache = jnp.dot(place, arrived, preferred_element_type=F32).astype(BF16)
    return (hidden_out, kv_cache.reshape(pages_dev, PAGE, kv_local, 2 * HD))


def solution(mesh):
    return jax.shard_map(
        local,
        mesh=mesh,
        in_specs=(
            P("req", None),
            P("req", None),
            P("req", None),
            P(),
            P(),
            P(None, "tp"),
            P(None, "tp"),
            P(None, "tp"),
            P("tp", None),
        ),
        out_specs=(P("req", "tp"), P("req", None, "tp", None)),
        check_vma=False,
    )
```

profile of v0, /device:TPU:0, one launch (start us, length us, event | category | flops | bytes accessed | tf_op | source)
XLA Modules:
  0.0 194.6 jit_solution(2767743607340653461)
XLA Ops:
  0.7 3.6 %multiply_reduce_fusion = f32[1024]{0:T(1024)S(1)} fusion(bf16[1024,2560]{1,0:T(8,128)(2,1)} %param.9), kind=kLoop, calls=%fused_computation | loop fusion | flops 7863296 | bytes 5246976 | tf_op jit(solution)/shard_map/reduce_sum | solution.py:170
  4.5 3.5 %multiply_convert_fusion = (bf16[1024,640]{1,0:T(8,128)(2,1)}, bf16[1024,640]{1,0:T(8,128)(2,1)S(1)}) fusion(f32[640]{0:T(1024)S(1)} %get-tuple-element.36, bf16[1024,2560]{1,0:T(8,128)(2,1)} %param.9, s32[]{:T(128)S(6)} %select_n.56, f32[1024]{0:T(1024)S(1)} %add_rsqrt_fusion, f32[640]{0:T(1024)S(1)} %get-tuple-element.37, s32[]{:T(128)S(6)} %select_n.55), kind=kLoop, calls=%fused_computation.19 | loop fusion | flops 5242880 | bytes 5252104 | tf_op jit(solution)/shard_map/convert_element_type | solution.py:175
  7.9 2.2 %fusion.9 = bf16[640,640]{1,0:T(8,128)(2,1)} fusion(bf16[1024,640]{1,0:T(8,128)(2,1)S(1)} %get-tuple-element.23, s32[640]{0:T(1024)S(1)} %eq.126), kind=kOutput, calls=%fused_computation.33 | convolution fusion | flops 839925760 | bytes 2132480 | tf_op jit(solution)/shard_map/dot_general | solution.py:183
  10.1 7.3 %all-to-all-start = ((bf16[8,80,640]{2,1,0:T(8,128)(2,1)}), bf16[8,80,640]{2,1,0:T(8,128)(2,1)}, u32[]{:S(2)}, u32[]{:S(2)}) async-start(bf16[8,80,640]{2,1,0:T(8,128)(2,1)} %bitcast.1), calls=%async_computation | async-start | bytes 1638400 | tf_op jit(solution)/shard_map/all_to_all | solution.py:187
  17.5 4.0 %copy.17 = bf16[2560,640]{0,1:T(8,128)(2,1)S(1)} copy(bf16[2560,640]{1,0:T(8,128)(2,1)} %param.14) | data formatting | bytes 6553600 | tf_op args[5]
  21.6 2.9 %pad.26 = bf16[2560,8,2,64]{0,3,2,1:T(8,128)(2,1)} pad(bf16[2560,8,2,40]{0,3,2,1:T(8,128)(2,1)S(1)} %bitcast.49, bf16[]{:T(256)} %constant.81.clone.1), padding=0_0x0_0x0_0x0_24 | pad | bytes 8519682 | tf_op jit(solution)/shard_map/jit(_pad)/pad | solution.py:27
  28.9 2.2 %constant_dynamic-slice_fusion.2 = (bf16[640,640]{1,0:T(8,128)(2,1)S(1)}, bf16[640,640]{1,0:T(8,128)(2,1)S(1)}, bf16[640,640]{1,0:T(8,128)(2,1)S(1)}, bf16[640,640]{1,0:T(8,128)(2,1)S(1)}) fusion(bf16[640,2560]{1,0:T(8,128)(2,1)} %param.17, s32[]{:T(128)S(6)} %select_n.57, s32[]{:T(128)S(6)} %select_n.56, s32[]{:T(128)S(6)} %select_n.55, s32[]{:T(128)S(6)} %select_n.58), kind=kLoop, calls=%fused_computation.69 | loop fusion | bytes 6553616 | tf_op jit(solution)/shard_map/dynamic_slice | solution.py:195
  35.2 2.2 %convolution_convert_fusion.4 = bf16[384,1280]{1,0:T(8,128)(2,1)} fusion(bf16[1024,640]{1,0:T(8,128)(2,1)S(1)} %copy-done.7, bf16[1024,640]{1,0:T(8,128)(2,1)S(1)} %copy-done.9, s32[384]{0:T(512)S(1)} %eq.130), kind=kOutput, calls=%fused_computation.12 | convolution fusion | flops 1012760576 | bytes 3606016 | tf_op jit(solution)/shard_map/dot_general | solution.py:183
  38.4 5.0 %all-to-all-start.1 = ((bf16[8,48,1280]{2,1,0:T(8,128)(2,1)}), bf16[8,48,1280]{2,1,0:T(8,128)(2,1)}, u32[]{:S(2)}, u32[]{:S(2)}) async-start(bf16[8,48,1280]{2,1,0:T(8,128)(2,1)} %bitcast.62), calls=%async_computation.1 | async-start | bytes 1966080 | tf_op jit(solution)/shard_map/all_to_all | solution.py:187
  45.0 6.5 %pad_maximum_fusion = bf16[2560,1536]{0,1:T(8,128)(2,1)} fusion(bf16[2560,256]{0,1:T(8,128)(2,1)} %bitcast.53, bf16[2560,256]{0,1:T(8,128)(2,1)S(1)} %bitcast.52, bf16[2560,1024]{0,1:T(8,128)(2,1)} %bitcast.48), kind=kLoop, calls=%fused_computation.1 | loop fusion | flops 23592960 | bytes 15728640 | tf_op jit(solution)/shard_map/concatenate | solution.py:189
  51.5 11.4 %collective-permute-done = bf16[640,640]{1,0:T(8,128)(2,1)S(1)} collective-permute-done((bf16[640,640]{1,0:T(8,128)(2,1)}, bf16[640,640]{1,0:T(8,128)(2,1)S(1)}, u32[]{:S(2)}, u32[]{:S(2)}) %collective-permute-start) | collective-permute-done | bytes 819232 | tf_op jit(solution)/shard_map/ppermute | solution.py:160
  64.8 2.7 %all-to-all-done.1 = bf16[8,48,1280]{2,1,0:T(8,128)(2,1)} async-done(((bf16[8,48,1280]{2,1,0:T(8,128)(2,1)}), bf16[8,48,1280]{2,1,0:T(8,128)(2,1)}, u32[]{:S(2)}, u32[]{:S(2)}) %all-to-all-start.1) | async-done | bytes 983072 | tf_op jit(solution)/shard_map/all_to_all | solution.py:187
  67.5 4.0 %constant_dynamic-slice_fusion.8 = (bf16[640,1536]{0,1:T(8,128)(2,1)S(1)}, bf16[640,1536]{0,1:T(8,128)(2,1)S(1)}, bf16[640,1536]{0,1:T(8,128)(2,1)S(1)}, bf16[640,1536]{0,1:T(8,128)(2,1)S(1)}) fusion(bf16[2560,1536]{0,1:T(8,128)(2,1)} %pad_maximum_fusion, s32[]{:T(128)S(6)} %select_n.55, s32[]{:T(128)S(6)} %select_n.58, s32[]{:T(128)S(6)} %select_n.57, ...), kind=kLoop, calls=%fused_computation.75 | loop fusion | bytes 15728656 | tf_op jit(solution)/shard_map/dynamic_slice | solution.py:193
  71.6 2.9 %fusion.6 = f32[384,1536]{1,0:T(8,128)S(1)} fusion(bf16[384,1280]{1,0:T(8,128)(2,1)} %bitcast.10, bf16[640,1536]{0,1:T(8,128)(2,1)S(1)} %get-tuple-element.21, bf16[640,1536]{0,1:T(8,128)(2,1)S(1)} %get-tuple-element.18), kind=kOutput, calls=%fused_computation.24 | convolution fusion | flops 1517813760 | bytes 7274496 | tf_op jit(solution)/shard_map/dot_general | solution.py:207
  76.3 4.2 %fusion.5 = f32[640,1536]{1,0:T(8,128)S(1)} fusion(bf16[640,1280]{1,0:T(8,128)(2,1)} %collective-permute-done.1, bf16[640,1536]{0,1:T(8,128)(2,1)S(1)} %get-tuple-element.19, bf16[640,1536]{0,1:T(8,128)(2,1)S(1)} %get-tuple-element.20), kind=kOutput, calls=%fused_computation.23 | convolution fusion | flops 2524446720 | bytes 9502720 | tf_op jit(solution)/shard_map/dot_general | solution.py:210
  80.5 3.9 %convolution_add_fusion.refs_0_ = f32[640,1536]{1,0:T(8,128)S(1)} fusion(f32[640,1536]{1,0:T(8,128)S(1)} %fusion.5, bf16[640,1536]{0,1:T(8,128)(2,1)S(1)} %get-tuple-element.21, bf16[640,1536]{0,1:T(8,128)(2,1)S(1)} %get-tuple-element.18, bf16[640,640]{1,0:T(8,128)(2,1)S(1)} %copy-done.13, bf16[640,640]{1,0:T(8,128)(2,1)} %bitcast.2), kind=kOutput, calls=%fused_computation.8 | convolution fusion | flops 2528706560 | bytes 13434880 | tf_op jit(solution)/shard_map/dot_general | solution.py:207
  84.5 18.3 %shard_map.104 = (bf16[512,1024]{1,0:T(8,128)(2,1)S(1)}, bf16[512,1024]{1,0:T(8,128)(2,1)S(1)}, bf16[1024,256]{1,0:T(8,128)(2,1)S(1)}, bf16[1024,256]{1,0:T(8,128)(2,1)S(1)}) custom-call(f32[640,1536]{1,0:T(8,128)S(1)} %convolution_add_fusion.refs_0_, f32[384,1536]{1,0:T(8,128)S(1)} %convolution_add_fusion.1.refs_1_, f32[1024,128]{1,0:T(8,128)S(1)} %copy.18.refs_2_, ...), custom_call_target="tpu_custom_call" | custom-call | flops 2684354560 | bytes 10485760 | tf_op jit(solution)/shard_map/pallas_call | solution.py:118
  102.8 2.6 %convolution_convert_fusion.2 = bf16[512,1280]{1,0:T(8,128)(2,1)} fusion(bf16[512,1024]{1,0:T(8,128)(2,1)S(1)} %get-tuple-element.11, bf16[1024,1280]{1,0:T(8,128)(2,1)S(1)} %bitcast.54), kind=kOutput, calls=%fused_computation.9 | convolution fusion | flops 1342832640 | bytes 4980736 | tf_op jit(solution)/shard_map/dot_general | solution.py:224
  105.9 2.6 %convolution_convert_fusion.3 = bf16[512,1280]{1,0:T(8,128)(2,1)} fusion(bf16[512,1024]{1,0:T(8,128)(2,1)S(1)} %get-tuple-element.10, bf16[1024,1280]{1,0:T(8,128)(2,1)S(1)} %bitcast.55), kind=kOutput, calls=%fused_computation.10 | convolution fusion | flops 1342832640 | bytes 4980736 | tf_op jit(solution)/shard_map/dot_general | solution.py:224
  108.6 3.1 %pad.31 = bf16[8,128,1280]{2,1,0:T(8,128)(2,1)} pad(bf16[8,80,1280]{2,1,0:T(8,128)(2,1)} %bitcast.50, bf16[]{:T(256)} %constant.81.clone.1), padding=0_0x0_48x0_0 | pad | bytes 4259842 | tf_op jit(solution)/shard_map/jit(_pad)/pad | solution.py:35
  112.0 3.2 %concatenate.40 = bf16[1024,320]{1,0:T(8,128)(2,1)S(1)} concatenate(bf16[1024,40]{1,0:T(8,128)(2,1)S(1)} %get-tuple-element.33, bf16[1024,40]{1,0:T(8,128)(2,1)S(1)} %get-tuple-element.32, bf16[1024,80]{1,0:T(8,128)(2,1)S(1)} %get-tuple-element.29, bf16[1024,40]{1,0:T(8,128)(2,1)S(1)} %get-tuple-element.31, bf16[1024,40]{1,0:T(8,128)(2,1)S(1)} %get-tuple-element.30, ...), dimensions={1} | concatenate | bytes 1310720 | tf_op jit(solution)/shard_map/concatenate | solution.py:267
  117.1 3.6 %all-to-all-start.4 = ((bf16[8,8,5120]{2,1,0:T(8,128)(2,1)}), bf16[8,8,5120]{2,1,0:T(8,128)(2,1)S(1)}, u32[]{:S(2)}, u32[]{:S(2)}) async-start(bf16[8,8,5120]{2,1,0:T(8,128)(2,1)} %fusion), calls=%async_computation.4 | async-start | bytes 1310720 | tf_op jit(solution)/shard_map/all_to_all | solution.py:273
  120.7 3.8 %convert_add_fusion = f32[512,1280]{1,0:T(8,128)S(1)} fusion(bf16[512,1280]{1,0:T(8,128)(2,1)} %collective-permute-done.4, bf16[512,1024]{1,0:T(8,128)(2,1)S(1)} %copy-done.3, bf16[1024,1280]{1,0:T(8,128)(2,1)} %bitcast.56), kind=kOutput, calls=%fused_computation.17 | convolution fusion | flops 1343488000 | bytes 7602176 | tf_op jit(solution)/shard_map/dot_general | solution.py:228
  124.6 3.8 %convert_add_fusion.1 = f32[512,1280]{1,0:T(8,128)S(1)} fusion(bf16[512,1280]{1,0:T(8,128)(2,1)} %collective-permute-done.3, bf16[512,1024]{1,0:T(8,128)(2,1)S(1)} %copy-done.1, bf16[1024,1280]{1,0:T(8,128)(2,1)S(1)} %bitcast.57), kind=kOutput, calls=%fused_computation.18 | convolution fusion | flops 1343488000 | bytes 7602176 | tf_op jit(solution)/shard_map/dot_general | solution.py:228
  130.2 15.6 %collective-permute-done.5 = bf16[512,640]{1,0:T(8,128)(2,1)S(1)} collective-permute-done((bf16[512,640]{1,0:T(8,128)(2,1)S(1)}, bf16[512,640]{1,0:T(8,128)(2,1)S(1)}, u32[]{:S(2)}, u32[]{:S(2)}) %collective-permute-start.5) | collective-permute-done | bytes 655392 | tf_op jit(solution)/shard_map/ppermute | solution.py:160
  146.8 5.7 %all-to-all-start.2 = ((bf16[8,64,640]{2,1,0:T(8,128)(2,1)}), bf16[8,64,640]{2,1,0:T(8,128)(2,1)S(1)}, u32[]{:S(2)}, u32[]{:S(2)}) async-start(bf16[8,64,640]{2,1,0:T(8,128)(2,1)} %bitcast.21), calls=%async_computation.2 | async-start | bytes 1310720 | tf_op jit(solution)/shard_map/all_to_all | solution.py:241
  153.9 14.2 %collective-permute-done.6 = bf16[512,640]{1,0:T(8,128)(2,1)S(1)} collective-permute-done((bf16[512,640]{1,0:T(8,128)(2,1)S(1)}, bf16[512,640]{1,0:T(8,128)(2,1)S(1)}, u32[]{:S(2)}, u32[]{:S(2)}) %collective-permute-start.6) | collective-permute-done | bytes 655392 | tf_op jit(solution)/shard_map/ppermute | solution.py:160
  169.3 5.6 %all-to-all-start.3 = ((bf16[8,64,640]{2,1,0:T(8,128)(2,1)}), bf16[8,64,640]{2,1,0:T(8,128)(2,1)S(1)}, u32[]{:S(2)}, u32[]{:S(2)}) async-start(bf16[8,64,640]{2,1,0:T(8,128)(2,1)} %bitcast.23), calls=%async_computation.3 | async-start | bytes 1310720 | tf_op jit(solution)/shard_map/all_to_all | solution.py:241
  175.6 2.2 %reshape.128 = bf16[64,16,2,160]{3,2,1,0:T(2,128)(2,1)} reshape(bf16[64,5120]{1,0:T(8,128)(2,1)S(1)} %convolution_convert_fusion) | data formatting | bytes 1310720 | tf_op jit(solution)/shard_map/reshape | solution.py:282
  177.8 2.6 %fusion.7 = f32[1024,640]{1,0:T(8,128)} fusion(bf16[512,640]{1,0:T(8,128)(2,1)S(1)} %bitcast.65, s32[512]{0:T(512)S(1)} %eq.122), kind=kOutput, calls=%fused_computation.27 | convolution fusion | flops 671612928 | bytes 3278848 | tf_op jit(solution)/shard_map/dot_general | solution.py:245
  180.4 9.9 %all-to-all-done.3 = bf16[8,64,640]{2,1,0:T(8,128)(2,1)S(1)} async-done(((bf16[8,64,640]{2,1,0:T(8,128)(2,1)}), bf16[8,64,640]{2,1,0:T(8,128)(2,1)S(1)}, u32[]{:S(2)}, u32[]{:S(2)}) %all-to-all-start.3) | async-done | bytes 655392 | tf_op jit(solution)/shard_map/all_to_all | solution.py:241
  190.3 4.3 %add_convert_fusion = bf16[1024,640]{1,0:T(8,128)(2,1)} fusion(f32[1024,640]{1,0:T(8,128)} %fusion.7, bf16[512,640]{1,0:T(8,128)(2,1)S(1)} %bitcast.66, bf16[1024,2560]{1,0:T(8,128)(2,1)} %param.9, s32[]{:T(128)S(6)} %select_n.52, s32[512]{0:T(512)S(1)} %eq.134), kind=kOutput, calls=%fused_computation.16 | convolution fusion | flops 674234368 | bytes 5900292 | tf_op jit(solution)/shard_map/dot_general | solution.py:245
  (95 shorter events, 24.0 us)
Async XLA Ops:
  0.7 3.6 %copy-start.14 = (s32[1,1024]{1,0:T(1,128)S(1)}, s32[1,1024]{1,0:T(1,128)}, u32[]{:S(2)}) copy-start(s32[1,1024]{1,0:T(1,128)} %param.11) | copy-start | bytes 12292
  0.7 3.7 %copy-start.17 = (bf16[2560]{0:T(1024)(128)(2,1)S(1)}, bf16[2560]{0:T(1024)(128)(2,1)}, u32[]{:S(2)}) copy-start(bf16[2560]{0:T(1024)(128)(2,1)} %param.13) | copy-start | bytes 15364
  7.9 2.2 %copy-start.8 = (bf16[1024,640]{1,0:T(8,128)(2,1)}, bf16[1024,640]{1,0:T(8,128)(2,1)S(1)}, u32[]{:S(2)}) copy-start(bf16[1024,640]{1,0:T(8,128)(2,1)S(1)} %get-tuple-element.23) | copy-start | bytes 3932164
  10.1 28.3 %all-to-all-start = ((bf16[8,80,640]{2,1,0:T(8,128)(2,1)}), bf16[8,80,640]{2,1,0:T(8,128)(2,1)}, u32[]{:S(2)}, u32[]{:S(2)}) async-start(bf16[8,80,640]{2,1,0:T(8,128)(2,1)} %bitcast.1), calls=%async_computation | async-start | bytes 1638400 | tf_op jit(solution)/shard_map/all_to_all | solution.py:187
  21.5 2.9 %copy-start.10 = (bf16[2560,160]{0,1:T(8,128)(2,1)S(1)}, bf16[2560,160]{0,1:T(8,128)(2,1)}, u32[]{:S(2)}) copy-start(bf16[2560,160]{0,1:T(8,128)(2,1)} %param.15) | copy-start | bytes 2457604
  24.5 1.1 copy-start.11
  24.5 2.4 %copy-start.15 = (s32[1,1024]{1,0:T(1,128)S(1)}, s32[1,1024]{1,0:T(1,128)}, u32[]{:S(2)}) copy-start(s32[1,1024]{1,0:T(1,128)} %param.10) | copy-start | bytes 12292
  32.5 1.8 copy-start.7
  32.5 2.7 %copy-start.9 = (bf16[1024,640]{1,0:T(8,128)(2,1)S(1)}, bf16[1024,640]{1,0:T(8,128)(2,1)}, u32[]{:S(2)}) copy-start(bf16[1024,640]{1,0:T(8,128)(2,1)} %copy-done.8) | copy-start | bytes 3932164
  35.2 8.3 %copy-start.16 = (s32[8,64]{1,0:T(8,128)S(1)}, s32[8,64]{1,0:T(8,128)}, u32[]{:S(2)}) copy-start(s32[8,64]{1,0:T(8,128)} %param.12) | copy-start | bytes 6148
  38.4 29.1 %all-to-all-start.1 = ((bf16[8,48,1280]{2,1,0:T(8,128)(2,1)}), bf16[8,48,1280]{2,1,0:T(8,128)(2,1)}, u32[]{:S(2)}, u32[]{:S(2)}) async-start(bf16[8,48,1280]{2,1,0:T(8,128)(2,1)} %bitcast.62), calls=%async_computation.1 | async-start | bytes 1966080 | tf_op jit(solution)/shard_map/all_to_all | solution.py:187
  43.4 19.4 %collective-permute-start = (bf16[640,640]{1,0:T(8,128)(2,1)}, bf16[640,640]{1,0:T(8,128)(2,1)S(1)}, u32[]{:S(2)}, u32[]{:S(2)}) collective-permute-start(bf16[640,640]{1,0:T(8,128)(2,1)} %bitcast.2), channel_id=1, source_target_pairs={{2,0},{3,1},{0,2},{1,3},{6,4},{7,5},{4,6},{5,7},{10,8},{11,9},{8,1... | collective-permute-start | bytes 2457608 | tf_op jit(solution)/shard_map/ppermute | solution.py:160
  62.9 1.6 copy-start.12
  64.4 11.8 %collective-permute-start.1 = (bf16[640,1280]{1,0:T(8,128)(2,1)S(1)}, bf16[640,1280]{1,0:T(8,128)(2,1)}, u32[]{:S(2)}, u32[]{:S(2)}) collective-permute-start(bf16[640,1280]{1,0:T(8,128)(2,1)S(1)} %pad_maximum_fusion.7), channel_id=1, source_target_pairs={{1,0},{0,1},{3,2},{2,3},{5,4},{4,5},{7,6},{6,7},{9,8},{8,9},{11,10... | collective-permute-start | bytes 4915208 | tf_op jit(solution)/shard_map/ppermute | solution.py:164
  67.5 7.0 %collective-permute-start.2 = (bf16[384,1280]{1,0:T(8,128)(2,1)}, bf16[384,1280]{1,0:T(8,128)(2,1)S(1)}, u32[]{:S(2)}, u32[]{:S(2)}) collective-permute-start(bf16[384,1280]{1,0:T(8,128)(2,1)} %bitcast.10), channel_id=1, source_target_pairs={{1,0},{0,1},{3,2},{2,3},{5,4},{4,5},{7,6},{6,7},{9,8},{8,9},{11,10... | collective-permute-start | bytes 2949128 | tf_op jit(solution)/shard_map/ppermute | solution.py:164
  76.3 4.3 %copy-start.13 = (bf16[640,640]{1,0:T(8,128)(2,1)S(1)}, bf16[640,640]{1,0:T(8,128)(2,1)}, u32[]{:S(2)}) copy-start(bf16[640,640]{1,0:T(8,128)(2,1)} %copy-done.12) | copy-start | bytes 2457604
  84.5 18.3 %copy-start.5 = (bf16[8,128,1280]{2,1,0:T(8,128)(2,1)S(1)}, bf16[8,128,1280]{2,1,0:T(8,128)(2,1)}, u32[]{:S(2)}) copy-start(bf16[8,128,1280]{2,1,0:T(8,128)(2,1)} %pad.32) | copy-start | bytes 7864324
  102.8 2.7 %copy-start.2 = (bf16[512,1024]{1,0:T(8,128)(2,1)}, bf16[512,1024]{1,0:T(8,128)(2,1)S(1)}, u32[]{:S(2)}) copy-start(bf16[512,1024]{1,0:T(8,128)(2,1)S(1)} %get-tuple-element.11) | copy-start | bytes 3145732
  102.8 3.2 %copy-start = (bf16[512,1024]{1,0:T(8,128)(2,1)}, bf16[512,1024]{1,0:T(8,128)(2,1)S(1)}, u32[]{:S(2)}) copy-start(bf16[512,1024]{1,0:T(8,128)(2,1)S(1)} %get-tuple-element.10) | copy-start | bytes 3145732
  105.4 15.3 %collective-permute-start.4 = (bf16[512,1280]{1,0:T(8,128)(2,1)}, bf16[512,1280]{1,0:T(8,128)(2,1)}, u32[]{:S(2)}, u32[]{:S(2)}) collective-permute-start(bf16[512,1280]{1,0:T(8,128)(2,1)} %convolution_convert_fusion.2), channel_id=1, source_target_pairs={{1,0},{0,1},{3,2},{2,3},{5,4},{4,5},{7,6},{6,7},{9,8},{8,9},{11,10... | collective-permute-start | bytes 3932168 | tf_op jit(solution)/shard_map/ppermute | solution.py:164
  108.5 16.0 %collective-permute-start.3 = (bf16[512,1280]{1,0:T(8,128)(2,1)}, bf16[512,1280]{1,0:T(8,128)(2,1)}, u32[]{:S(2)}, u32[]{:S(2)}) collective-permute-start(bf16[512,1280]{1,0:T(8,128)(2,1)} %convolution_convert_fusion.3), channel_id=1, source_target_pairs={{1,0},{0,1},{3,2},{2,3},{5,4},{4,5},{7,6},{6,7},{9,8},{8,9},{11,10... | collective-permute-start | bytes 3932168 | tf_op jit(solution)/shard_map/ppermute | solution.py:164
  115.2 5.5 %copy-start.3 = (bf16[512,1024]{1,0:T(8,128)(2,1)S(1)}, bf16[512,1024]{1,0:T(8,128)(2,1)}, u32[]{:S(2)}) copy-start(bf16[512,1024]{1,0:T(8,128)(2,1)} %copy-done.2) | copy-start | bytes 3145732
  117.1 29.6 %all-to-all-start.4 = ((bf16[8,8,5120]{2,1,0:T(8,128)(2,1)}), bf16[8,8,5120]{2,1,0:T(8,128)(2,1)S(1)}, u32[]{:S(2)}, u32[]{:S(2)}) async-start(bf16[8,8,5120]{2,1,0:T(8,128)(2,1)} %fusion), calls=%async_computation.4 | async-start | bytes 1310720 | tf_op jit(solution)/shard_map/all_to_all | solution.py:273
  120.7 3.8 %copy-start.1 = (bf16[512,1024]{1,0:T(8,128)(2,1)S(1)}, bf16[512,1024]{1,0:T(8,128)(2,1)}, u32[]{:S(2)}) copy-start(bf16[512,1024]{1,0:T(8,128)(2,1)} %copy-done) | copy-start | bytes 3145732
  120.7 3.8 %copy-start.6 = (bf16[8,128,1280]{2,1,0:T(8,128)(2,1)S(1)}, bf16[8,128,1280]{2,1,0:T(8,128)(2,1)}, u32[]{:S(2)}) copy-start(bf16[8,128,1280]{2,1,0:T(8,128)(2,1)} %pad.31) | copy-start | bytes 7864324
  124.5 3.8 %copy-start.4 = (f32[512,1280]{1,0:T(8,128)}, f32[512,1280]{1,0:T(8,128)S(1)}, u32[]{:S(2)}) copy-start(f32[512,1280]{1,0:T(8,128)S(1)} %convert_add_fusion) | copy-start | bytes 7864324
  128.5 39.6 %slice-start = ((f32[512,1280]{1,0:T(8,128)}), f32[512,640]{1,0:T(8,128)S(1)}, s32[]{:S(2)}) async-start(f32[512,1280]{1,0:T(8,128)} %copy-done.4), calls=%async_computation.5 | async-start | bytes 2621440 | tf_op jit(solution)/shard_map/slice | solution.py:234
  128.6 17.2 %collective-permute-start.5 = (bf16[512,640]{1,0:T(8,128)(2,1)S(1)}, bf16[512,640]{1,0:T(8,128)(2,1)S(1)}, u32[]{:S(2)}, u32[]{:S(2)}) collective-permute-start(bf16[512,640]{1,0:T(8,128)(2,1)S(1)} %slice.71), channel_id=1, source_target_pairs={{2,0},{3,1},{0,2},{1,3},{6,4},{7,5},{4,6},{5,7},{10,8},{11,9},{8,1... | collective-permute-start | bytes 1966088 | tf_op jit(solution)/shard_map/ppermute | solution.py:160
  146.8 22.5 %all-to-all-start.2 = ((bf16[8,64,640]{2,1,0:T(8,128)(2,1)}), bf16[8,64,640]{2,1,0:T(8,128)(2,1)S(1)}, u32[]{:S(2)}, u32[]{:S(2)}) async-start(bf16[8,64,640]{2,1,0:T(8,128)(2,1)} %bitcast.21), calls=%async_computation.2 | async-start | bytes 1310720 | tf_op jit(solution)/shard_map/all_to_all | solution.py:241
  152.4 15.7 %collective-permute-start.6 = (bf16[512,640]{1,0:T(8,128)(2,1)S(1)}, bf16[512,640]{1,0:T(8,128)(2,1)S(1)}, u32[]{:S(2)}, u32[]{:S(2)}) collective-permute-start(bf16[512,640]{1,0:T(8,128)(2,1)S(1)} %slice.70), channel_id=1, source_target_pairs={{2,0},{3,1},{0,2},{1,3},{6,4},{7,5},{4,6},{5,7},{10,8},{11,9},{8,1... | collective-permute-start | bytes 1966088 | tf_op jit(solution)/shard_map/ppermute | solution.py:160
  169.3 21.0 %all-to-all-start.3 = ((bf16[8,64,640]{2,1,0:T(8,128)(2,1)}), bf16[8,64,640]{2,1,0:T(8,128)(2,1)S(1)}, u32[]{:S(2)}, u32[]{:S(2)}) async-start(bf16[8,64,640]{2,1,0:T(8,128)(2,1)} %bitcast.23), calls=%async_computation.3 | async-start | bytes 1310720 | tf_op jit(solution)/shard_map/all_to_all | solution.py:241
where the time goes:
time: 196 us; the launch traced here: 195 us
  waiting for transfers between devices  55 us (28%)
  matrix products  38.5 us (20%)
  starting transfers between devices  32.3 us (16%)
  local copies, waits for them, and re-layouts  29.1 us (15%)
  other arithmetic  20.3 us (10%)
  Pallas kernels  18.3 us (9%)
    ppermute x3, waiting for transfers between devices, from_x(): return lax.ppermute(array, 'tp', pairs)  41.2 us
    pallas_call x1, Pallas kernels, attention(): pl.pallas_call(functools.partial(attention_kernel, cuts, groups, heads, k...  18.3 us
    all_to_all x2, starting transfers between devices, deal(): return lax.all_to_all(sent, 'req', split_axis=0, concat_axis=0, tiled=True)  12.2 us
    all_to_all x2, starting transfers between devices, local(): lax.all_to_all(summed.astype(BF16), 'req', split_axis=0, concat_axis=0, t...  11.2 us
    all_to_all x2, waiting for transfers between devices, local(): lax.all_to_all(summed.astype(BF16), 'req', split_axis=0, concat_axis=0, t...  10 us
    dot_general x2, matrix products, local(): kept = jnp.dot(rows, out_keep, preferred_element_type=F32)  7.55 us
    dot_general x2, matrix products, local(): lax.dot_general(back, returned, (((0,), (0,)), ((), ())), preferred_eleme...  6.89 us
    dot_general x2, matrix products, local(): raw = jnp.dot(mine, weights[:half], preferred_element_type=F32)  6.83 us
  transfers between devices with their start and end apart: 12, of which 7 were waited for; matrix products, arithmetic and copies ran while one was open for 32% of the time, Pallas kernels for 0%

commit v1 on v0

--- a/solution.py
+++ b/solution.py
@@ -51,7 +51,7 @@
 def attention_kernel(cuts, groups, heads, kv, steps, *refs):
     raw_refs, refs = refs[: len(cuts)], refs[len(cuts) :]
     cos_ref, sin_ref, first_ref = refs[:3]
-    out_refs, refs = refs[3 : 3 + steps], refs[3 + steps :]
+    out_ref, refs = refs[3], refs[4:]
     key_ref, value_ref, query_scr, value_scr = refs
     share = cuts[-1][1]
     length = groups * share
@@ -106,13 +106,14 @@
             run = share // steps
             for block in range(tile // run):
                 g, step = divmod(low // run + block, steps)
-                out_refs[step][g * run : (g + 1) * run, mine] = done[block * run : (block + 1) * run]
+                at = (step * groups + g) * run
+                out_ref[at : at + run, mine] = done[block * run : (block + 1) * run]
 
 
 def attention(raw_parts, cuts, groups, heads, kv, steps, tables):
     cosine, sine, first_index = tables
     length = groups * cuts[-1][1]
-    shapes = [jax.ShapeDtypeStruct((length // steps, heads * LANES), BF16)] * steps
+    shapes = [jax.ShapeDtypeStruct((length, heads * LANES), BF16)]
     shapes += [jax.ShapeDtypeStruct((length, kv * LANES), BF16)] * 2
     whole = pl.BlockSpec(memory_space=pltpu.VMEM)
     outs = pl.pallas_call(
@@ -130,7 +131,125 @@
             transcendentals=length * 640 * heads,
         ),
     )(*raw_parts, cosine, sine, first_index[:, None])
-    return outs[:steps], outs[steps], outs[steps + 1]
+    return outs
+
+
+def return_kernel(
+    axes, kept_ref, leaving_ref, order_ref, hidden_ref, out_ref,
+    crossed, fin, ret, total, x_send, x_recv, r_send, r_recv,
+):
+    groups, xs, cores = axes
+    steps, _, run, part = kept_ref.shape
+    length = out_ref.shape[0]
+    me, tp = lax.axis_index("req"), lax.axis_index("tp")
+    my_x, my_core = tp // cores, tp % cores
+
+    def group(k):
+        return lax.rem(me + k, groups)
+
+    def along_x(k):
+        return lax.rem(my_x + k, xs) * cores + my_core
+
+    mesh_ids = pl.DeviceIdType.MESH
+    barrier = pltpu.get_barrier_semaphore()
+
+    @pl.loop(1, groups)
+    def _(k):
+        pl.semaphore_signal(barrier, inc=1, device_id=(group(k), tp), device_id_type=mesh_ids)
+
+    for k in range(1, xs):
+        pl.semaphore_signal(barrier, inc=1, device_id=(me, along_x(k)), device_id_type=mesh_ids)
+    pl.semaphore_wait(barrier, groups - 1 + xs - 1)
+
+    def x_copy(step, k):
+        return pltpu.make_async_remote_copy(
+            src_ref=leaving_ref.at[k - 1, step], dst_ref=crossed.at[k - 1, step],
+            send_sem=x_send.at[k - 1, step], recv_sem=x_recv.at[k - 1, step],
+            device_id=(me, along_x(k)), device_id_type=mesh_ids,
+        )
+
+    def ret_copy(step, k):
+        return pltpu.make_async_remote_copy(
+            src_ref=fin.at[step, group(k)], dst_ref=ret.at[step, me],
+            send_sem=r_send.at[step, k], recv_sem=r_recv.at[step, k],
+            device_id=(group(k), tp), device_id_type=mesh_ids,
+        )
+
+    def ret_arrival(step, k):
+        source = group(groups - k)
+        return pltpu.make_async_remote_copy(
+            src_ref=fin.at[step, source], dst_ref=ret.at[step, source],
+            send_sem=r_send.at[step, k], recv_sem=r_recv.at[step, k],
+            device_id=(group(k), tp), device_id_type=mesh_ids,
+        )
+
+    for step in range(steps):
+        for k in range(1, xs):
+            x_copy(step, k).start()
+    total[...] = hidden_ref[...].astype(F32)
+
+    def take(step):
+        @pl.loop(1, groups)
+        def _(k):
+            ret_arrival(step, k).wait_recv()
+
+        row = lax.broadcasted_iota(jnp.int32, (length, groups * run), 0)
+        back = (row == order_ref[step]).astype(F32).astype(BF16)
+        arrived = ret[step].reshape(groups * run, part)
+        total[...] += jnp.dot(back, arrived, preferred_element_type=F32)
+
+    for step in range(steps):
+        summed = kept_ref[step]
+        for k in range(1, xs):
+            x_copy(step, k).wait_recv()
+            summed = summed + crossed[k - 1, step].astype(F32)
+        fin[step] = summed.astype(BF16)
+
+        @pl.loop(1, groups)
+        def _(k):
+            ret_copy(step, k).start()
+
+        ret[step, me] = fin[step, me]
+        if step > 0:
+            take(step - 1)
+    take(steps - 1)
+    out_ref[...] = total[...].astype(BF16)
+
+    for step in range(steps):
+        for k in range(1, xs):
+            x_copy(step, k).wait_send()
+
+        @pl.loop(1, groups)
+        def _(k):
+            ret_copy(step, k).wait_send()
+
+
+def give_back(axes, kept, leaving, order, hidden_own):
+    groups, xs, _ = axes
+    steps, _, run, part = kept.shape
+    length = hidden_own.shape[0]
+    vmem = pl.BlockSpec(memory_space=pltpu.VMEM)
+    dma = pltpu.SemaphoreType.DMA
+    return pl.pallas_call(
+        functools.partial(return_kernel, axes),
+        out_shape=jax.ShapeDtypeStruct((length, part), BF16),
+        in_specs=[vmem] * 4,
+        out_specs=vmem,
+        scratch_shapes=[
+            pltpu.VMEM((xs - 1, steps, groups, run, part), BF16),
+            pltpu.VMEM((steps, groups, run, part), BF16),
+            pltpu.VMEM((steps, groups, run, part), BF16),
+            pltpu.VMEM((length, part), F32),
+            dma((xs - 1, steps)), dma((xs - 1, steps)),
+            dma((steps, groups)), dma((steps, groups)),
+        ],
+        compiler_params=pltpu.CompilerParams(
+            collective_id=0, has_side_effects=True, vmem_limit_bytes=40 * 2**20
+        ),
+        cost_estimate=pl.CostEstimate(
+            flops=2 * length * length * part, bytes_accessed=16 * 2**20, transcendentals=0
+        ),
+    )(kept, leaving, order, hidden_own)
 
 
 def one_hot_rows(index, count):
@@ -211,41 +330,24 @@
         raw_parts.append(raw)
 
     heads_local, kv_local = w_query.shape[1] // HD, w_key.shape[1] // HD
-    steps = 2 if share % 32 == 0 else 1
+    steps = 4 if share % 64 == 0 else 2 if share % 32 == 0 else 1
     attended, key_pad, value_pad = attention(
         raw_parts, cuts, groups, heads_local, kv_local, steps, rope_tables(segment_row)
     )
 
-    total = lax.dynamic_slice_in_dim(hidden, tp_place * part, part, 1).astype(F32)
-    kept_parts = []
-    came_parts = [None] * steps
+    run = share // steps
+    kept = jnp.dot(attended, out_keep, preferred_element_type=F32)
     if cores == 2:
-        came_parts = [
-            from_core(jnp.dot(rows, out_send, preferred_element_type=F32).astype(BF16))
-            for rows in attended
-        ]
-    for rows, came in zip(attended, came_parts):
-        kept = jnp.dot(rows, out_keep, preferred_element_type=F32)
-        kept_parts.append(kept if came is None else kept + came.astype(F32))
-    leaving_parts = [
-        [kept[:, k * part : (k + 1) * part].astype(BF16) for k in range(1, xs)]
-        for kept in kept_parts
-    ]
-    kept_parts = [kept[:, :part] for kept in kept_parts]
-    kept_parts, leaving_parts = lax.optimization_barrier((kept_parts, leaving_parts))
-    for step in range(steps):
-        low, high = step * share // steps, (step + 1) * share // steps
-        summed = kept_parts[step]
-        for k in range(1, xs):
-            summed = summed + from_x(leaving_parts[step][k - 1], xs - k).astype(F32)
-        returned = lax.all_to_all(
-            summed.astype(BF16), "req", split_axis=0, concat_axis=0, tiled=True
-        )
-        back = one_hot_rows(order_grid[:, low:high].reshape(-1), length)
-        total = total + lax.dot_general(
-            back, returned, (((0,), (0,)), ((), ())), preferred_element_type=F32
-        )
-    hidden_out = total.astype(BF16)
+        given = jnp.dot(attended, out_send, preferred_element_type=F32).astype(BF16)
+        kept = kept + from_core(given).astype(F32)
+    kept = kept.reshape(steps, groups, run, -1)
+    leaving = [kept[..., k * part : (k + 1) * part].astype(BF16) for k in range(1, xs)]
+    order_steps = order_grid.reshape(groups, steps, run).transpose(1, 0, 2)
+    hidden_out = give_back(
+        (groups, xs, cores), kept[..., :part], jnp.stack(leaving),
+        order_steps.reshape(steps, 1, groups * run),
+        lax.dynamic_slice_in_dim(hidden, tp_place * part, part, 1),
+    )
 
     pages_dev = length // PAGE
     per_owner = pages_dev // groups

time: 196 us -> 194 us (0.990)
  Pallas kernels: 18.3 us -> 57.9 us
  waiting for transfers between devices: 55 us -> 30.6 us
  starting transfers between devices: 32.3 us -> 18.7 us
  matrix products: 38.5 us -> 31.4 us
  local copies, waits for them, and re-layouts: 29.1 us -> 32.5 us
    pallas_call x0 -> x1, Pallas kernels: none -> 39.8 us  [give_back(): pl.pallas_call(functools.partial(return_kernel, axes), out_shape=jax.Shap...]
    ppermute x3 -> x1, waiting for transfers between devices: 41.2 us -> 11.4 us  [from_x(): return lax.ppermute(array, 'tp', pairs)]
    all_to_all x1, waiting for transfers between devices: 0.01 us -> 13.2 us  [local(): lax.all_to_all(page_rows, 'req', split_axis=0, concat_axis=0, tiled=True)]
    all_to_all x2 -> x0, starting transfers between devices: 11.2 us -> none  [local(): lax.all_to_all(summed.astype(BF16), 'req', split_axis=0, concat_axis=0, t...]
    dot_general x6 -> x2, matrix products: 19.6 us -> 9.55 us  [the longest x1 5.42 us: local(): kept = jnp.dot(attended, out_keep, preferred_element_type=F32)]
    all_to_all x2 -> x0, waiting for transfers between devices: 10 us -> none  [local(): lax.all_to_all(summed.astype(BF16), 'req', split_axis=0, concat_axis=0, t...]
    ppermute x3 -> x1, starting transfers between devices: 4.6 us -> 1.49 us  [from_x(): return lax.ppermute(array, 'tp', pairs)]
    reshape x1, local copies, waits for them, and re-layouts: 2.19 us -> 5.13 us  [local(): return (hidden_out, kv_cache.reshape(pages_dev, PAGE, kv_local, 2 * HD))]
  transfers between devices with their start and end apart: 12 -> 7, of which waited for: 7 -> 4; matrix products, arithmetic and copies ran while one was open for 32% -> 28% of each run, Pallas kernels for 0% -> 0%
where the time goes in v1:
time: 194 us; the launch traced here: 193 us
  Pallas kernels  57.9 us (30%)
  local copies, waits for them, and re-layouts  32.5 us (17%)
  matrix products  31.4 us (16%)
  waiting for transfers between devices  30.6 us (16%)
  other arithmetic  21.1 us (11%)
  starting transfers between devices  18.7 us (10%)
    pallas_call x1, Pallas kernels, give_back(): pl.pallas_call(functools.partial(return_kernel, axes), out_shape=jax.Shap...  39.8 us
    pallas_call x1, Pallas kernels, attention(): pl.pallas_call(functools.partial(attention_kernel, cuts, groups, heads, k...  18.1 us
    all_to_all x1, waiting for transfers between devices, local(): lax.all_to_all(page_rows, 'req', split_axis=0, concat_axis=0, tiled=True)  13.2 us
    all_to_all x2, starting transfers between devices, deal(): return lax.all_to_all(sent, 'req', split_axis=0, concat_axis=0, tiled=True)  11.7 us
    ppermute x1, waiting for transfers between devices, from_x(): return lax.ppermute(array, 'tp', pairs)  11.4 us
    dot_general x2, matrix products, local(): raw = raw + jnp.dot(other, weights[half:], preferred_element_type=F32)  7.13 us
    unnamed x33, local copies, waits for them, and re-layouts  7.02 us
    dot_general x2, matrix products, local(): raw = jnp.dot(mine, weights[:half], preferred_element_type=F32)  6.85 us
  transfers between devices with their start and end apart: 7, of which 4 were waited for; matrix products, arithmetic and copies ran while one was open for 28% of the time, Pallas kernels for 0%

profile of v1, /device:TPU:0, one launch (start us, length us, event | category | flops | bytes accessed | tf_op | source)
XLA Modules:
  0.0 193.2 jit_solution(13218730440309616582)
XLA Ops:
  0.7 3.6 %multiply_reduce_fusion = f32[1024]{0:T(1024)S(1)} fusion(bf16[1024,2560]{1,0:T(8,128)(2,1)} %param.9), kind=kLoop, calls=%fused_computation | loop fusion | flops 7863296 | bytes 5246976 | tf_op jit(solution)/shard_map/reduce_sum | solution.py:289
  4.5 3.5 %multiply_convert_fusion = (bf16[1024,640]{1,0:T(8,128)(2,1)}, bf16[1024,640]{1,0:T(8,128)(2,1)S(1)}) fusion(f32[640]{0:T(1024)S(1)} %get-tuple-element.26, bf16[1024,2560]{1,0:T(8,128)(2,1)} %param.9, s32[]{:T(128)S(6)} %select_n.55, f32[1024]{0:T(1024)S(1)} %add_rsqrt_fusion, f32[640]{0:T(1024)S(1)} %get-tuple-element.27, s32[]{:T(128)S(6)} %select_n.54), kind=kLoop, calls=%fused_computation.17 | loop fusion | flops 5242880 | bytes 5252104 | tf_op jit(solution)/shard_map/convert_element_type | solution.py:294
  7.9 2.2 %fusion.7 = bf16[640,640]{1,0:T(8,128)(2,1)} fusion(bf16[1024,640]{1,0:T(8,128)(2,1)S(1)} %get-tuple-element.13, s32[640]{0:T(1024)S(1)} %eq.92), kind=kOutput, calls=%fused_computation.27 | convolution fusion | flops 839925760 | bytes 2132480 | tf_op jit(solution)/shard_map/dot_general | solution.py:302
  10.1 7.3 %all-to-all-start = ((bf16[8,80,640]{2,1,0:T(8,128)(2,1)}), bf16[8,80,640]{2,1,0:T(8,128)(2,1)}, u32[]{:S(2)}, u32[]{:S(2)}) async-start(bf16[8,80,640]{2,1,0:T(8,128)(2,1)} %bitcast.1), calls=%async_computation | async-start | bytes 1638400 | tf_op jit(solution)/shard_map/all_to_all | solution.py:306
  17.5 4.0 %copy.19 = bf16[2560,640]{0,1:T(8,128)(2,1)S(1)} copy(bf16[2560,640]{1,0:T(8,128)(2,1)} %param.14) | data formatting | bytes 6553600 | tf_op args[5]
  21.5 2.9 %pad.26 = bf16[2560,8,2,64]{0,3,2,1:T(8,128)(2,1)} pad(bf16[2560,8,2,40]{0,3,2,1:T(8,128)(2,1)S(1)} %bitcast.45, bf16[]{:T(256)} %constant.81.clone.1), padding=0_0x0_0x0_0x0_24 | pad | bytes 8519682 | tf_op jit(solution)/shard_map/jit(_pad)/pad | solution.py:27
  26.4 2.3 %constant_dynamic-slice_fusion.3 = (bf16[640,640]{1,0:T(8,128)(2,1)S(1)}, bf16[640,640]{1,0:T(8,128)(2,1)S(1)}, bf16[640,640]{1,0:T(8,128)(2,1)S(1)}, bf16[640,640]{1,0:T(8,128)(2,1)S(1)}) fusion(bf16[640,2560]{1,0:T(8,128)(2,1)} %param.17, s32[]{:T(128)S(6)} %select_n.56, s32[]{:T(128)S(6)} %select_n.55, s32[]{:T(128)S(6)} %select_n.54, s32[]{:T(128)S(6)} %select_n.57), kind=kLoop, calls=%fused_computation.60 | loop fusion | bytes 6553616 | tf_op jit(solution)/shard_map/dynamic_slice | solution.py:314
  29.1 2.2 %convolution_convert_fusion.3 = bf16[384,1280]{1,0:T(8,128)(2,1)} fusion(bf16[1024,640]{1,0:T(8,128)(2,1)S(1)} %copy-done.3, bf16[1024,640]{1,0:T(8,128)(2,1)S(1)} %copy-done.5, s32[384]{0:T(512)S(1)} %eq.96), kind=kOutput, calls=%fused_computation.12 | convolution fusion | flops 1012760576 | bytes 3606016 | tf_op jit(solution)/shard_map/dot_general | solution.py:302
  31.3 1.9 %pad_maximum_fusion.8 = (bf16[640,1280]{1,0:T(8,128)(2,1)}, bf16[640,1280]{1,0:T(8,128)(2,1)}) fusion(bf16[640,640]{1,0:T(8,128)(2,1)S(1)} %get-tuple-element.15, bf16[640,640]{1,0:T(8,128)(2,1)S(1)} %get-tuple-element.16, bf16[640,640]{1,0:T(8,128)(2,1)S(1)} %get-tuple-element.17, bf16[640,640]{1,0:T(8,128)(2,1)S(1)} %get-tuple-element.14), kind=kLoop, calls=%fused_computation.24 | loop fusion | flops 6553600 | bytes 6553600 | tf_op jit(solution)/shard_map/concatenate | solution.py:315
  33.2 5.2 %all-to-all-done = bf16[8,80,640]{2,1,0:T(8,128)(2,1)} async-done(((bf16[8,80,640]{2,1,0:T(8,128)(2,1)}), bf16[8,80,640]{2,1,0:T(8,128)(2,1)}, u32[]{:S(2)}, u32[]{:S(2)}) %all-to-all-start) | async-done | bytes 819232 | tf_op jit(solution)/shard_map/all_to_all | solution.py:306
  38.4 4.4 %all-to-all-start.1 = ((bf16[8,48,1280]{2,1,0:T(8,128)(2,1)}), bf16[8,48,1280]{2,1,0:T(8,128)(2,1)}, u32[]{:S(2)}, u32[]{:S(2)}) async-start(bf16[8,48,1280]{2,1,0:T(8,128)(2,1)} %bitcast.58), calls=%async_computation.1 | async-start | bytes 1966080 | tf_op jit(solution)/shard_map/all_to_all | solution.py:306
  44.3 1.5 collective-permute-start
  45.8 6.3 %pad_maximum_fusion = bf16[2560,1536]{0,1:T(8,128)(2,1)} fusion(bf16[2560,256]{0,1:T(8,128)(2,1)S(1)} %bitcast.49, bf16[2560,256]{0,1:T(8,128)(2,1)S(1)} %bitcast.48, bf16[2560,1024]{0,1:T(8,128)(2,1)} %bitcast.44), kind=kLoop, calls=%fused_computation.1 | loop fusion | flops 23592960 | bytes 15728640 | tf_op jit(solution)/shard_map/concatenate | solution.py:308
  52.1 11.4 %collective-permute-done = bf16[640,640]{1,0:T(8,128)(2,1)S(1)} collective-permute-done((bf16[640,640]{1,0:T(8,128)(2,1)}, bf16[640,640]{1,0:T(8,128)(2,1)S(1)}, u32[]{:S(2)}, u32[]{:S(2)}) %collective-permute-start) | collective-permute-done | bytes 819232 | tf_op jit(solution)/shard_map/ppermute | solution.py:279
  63.5 2.6 %pad_maximum_fusion.7 = bf16[640,1280]{1,0:T(8,128)(2,1)} fusion(bf16[640,640]{1,0:T(8,128)(2,1)S(1)} %collective-permute-done, bf16[640,640]{1,0:T(8,128)(2,1)} %bitcast.2), kind=kLoop, calls=%fused_computation.23 | loop fusion | flops 3276800 | bytes 3276800 | tf_op jit(solution)/shard_map/concatenate | solution.py:322
  67.6 1.6 pad.32
  69.3 4.0 %constant_dynamic-slice_fusion.9 = (bf16[640,1536]{0,1:T(8,128)(2,1)S(1)}, bf16[640,1536]{0,1:T(8,128)(2,1)S(1)}, bf16[640,1536]{0,1:T(8,128)(2,1)S(1)}, bf16[640,1536]{0,1:T(8,128)(2,1)S(1)}) fusion(bf16[2560,1536]{0,1:T(8,128)(2,1)} %pad_maximum_fusion, s32[]{:T(128)S(6)} %select_n.54, s32[]{:T(128)S(6)} %select_n.57, s32[]{:T(128)S(6)} %select_n.56, ...), kind=kLoop, calls=%fused_computation.66 | loop fusion | bytes 15728656 | tf_op jit(solution)/shard_map/dynamic_slice | solution.py:312
  73.3 2.9 %fusion.6 = f32[384,1536]{1,0:T(8,128)S(1)} fusion(bf16[384,1280]{1,0:T(8,128)(2,1)} %bitcast.10, bf16[640,1536]{0,1:T(8,128)(2,1)S(1)} %get-tuple-element.11, bf16[640,1536]{0,1:T(8,128)(2,1)S(1)} %get-tuple-element.8), kind=kOutput, calls=%fused_computation.22 | convolution fusion | flops 1517813760 | bytes 7274496 | tf_op jit(solution)/shard_map/dot_general | solution.py:326
  76.2 3.0 %convolution_add_fusion.1.refs_1_ = f32[384,1536]{1,0:T(8,128)S(1)} fusion(f32[384,1536]{1,0:T(8,128)S(1)} %fusion.6, bf16[384,1280]{1,0:T(8,128)(2,1)} %collective-permute-done.2, bf16[640,1536]{0,1:T(8,128)(2,1)S(1)} %get-tuple-element.9, bf16[640,1536]{0,1:T(8,128)(2,1)S(1)} %get-tuple-element.10), kind=kOutput, calls=%fused_computation.11 | convolution fusion | flops 1518403584 | bytes 9633792 | tf_op jit(solution)/shard_map/dot_general | solution.py:329
  79.2 4.2 %fusion.5 = f32[640,1536]{1,0:T(8,128)S(1)} fusion(bf16[640,1280]{1,0:T(8,128)(2,1)} %collective-permute-done.1, bf16[640,1536]{0,1:T(8,128)(2,1)S(1)} %get-tuple-element.9, bf16[640,1536]{0,1:T(8,128)(2,1)S(1)} %get-tuple-element.10), kind=kOutput, calls=%fused_computation.21 | convolution fusion | flops 2524446720 | bytes 9502720 | tf_op jit(solution)/shard_map/dot_general | solution.py:329
  83.4 3.9 %convolution_add_fusion.refs_0_ = f32[640,1536]{1,0:T(8,128)S(1)} fusion(f32[640,1536]{1,0:T(8,128)S(1)} %fusion.5, bf16[640,1536]{0,1:T(8,128)(2,1)S(1)} %get-tuple-element.11, bf16[640,1536]{0,1:T(8,128)(2,1)S(1)} %get-tuple-element.8, bf16[640,640]{1,0:T(8,128)(2,1)S(1)} %collective-permute-done, bf16[640,640]{1,0:T(8,128)(2,1)} %bitcast.2), kind=kOutput, calls=%fused_computation.10 | convolution fusion | flops 2528706560 | bytes 13434880 | tf_op jit(solution)/shard_map/dot_general | solution.py:326
  87.3 18.1 %shard_map.104 = (bf16[1024,1024]{1,0:T(8,128)(2,1)S(1)}, bf16[1024,256]{1,0:T(8,128)(2,1)S(1)}, bf16[1024,256]{1,0:T(8,128)(2,1)S(1)}) custom-call(f32[640,1536]{1,0:T(8,128)S(1)} %convolution_add_fusion.refs_0_, f32[384,1536]{1,0:T(8,128)S(1)} %convolution_add_fusion.1.refs_1_, f32[1024,128]{1,0:T(8,128)S(1)} %copy.20.refs_2_, ...), custom_call_target="tpu_custom_call" | custom-call | flops 2684354560 | bytes 10485760 | tf_op jit(solution)/shard_map/pallas_call | solution.py:119
  105.4 4.1 %convolution_convert_fusion.2 = bf16[1024,1280]{1,0:T(8,128)(2,1)} fusion(bf16[1024,1024]{1,0:T(8,128)(2,1)S(1)} %get-tuple-element.5, bf16[1024,1280]{1,0:T(8,128)(2,1)S(1)} %bitcast.52), kind=kOutput, calls=%fused_computation.9 | convolution fusion | flops 2685665280 | bytes 7340032 | tf_op jit(solution)/shard_map/dot_general | solution.py:341
  110.8 3.4 %concatenate.40 = bf16[1024,320]{1,0:T(8,128)(2,1)S(1)} concatenate(bf16[1024,40]{1,0:T(8,128)(2,1)S(1)} %get-tuple-element.23, bf16[1024,40]{1,0:T(8,128)(2,1)S(1)} %get-tuple-element.22, bf16[1024,80]{1,0:T(8,128)(2,1)S(1)} %get-tuple-element.19, bf16[1024,40]{1,0:T(8,128)(2,1)S(1)} %get-tuple-element.21, bf16[1024,40]{1,0:T(8,128)(2,1)S(1)} %get-tuple-element.20, ...), dimensions={1} | concatenate | bytes 1310720 | tf_op jit(solution)/shard_map/concatenate | solution.py:369
  116.0 5.0 %all-to-all-start.2 = ((bf16[8,8,5120]{2,1,0:T(8,128)(2,1)}), bf16[8,8,5120]{2,1,0:T(8,128)(2,1)}, u32[]{:S(2)}, u32[]{:S(2)}) async-start(bf16[8,8,5120]{2,1,0:T(8,128)(2,1)} %fusion), calls=%async_computation.2 | async-start | bytes 1310720 | tf_op jit(solution)/shard_map/all_to_all | solution.py:375
  121.2 1.7 pad.31
  124.3 1.6 constant_dynamic-slice_fusion.1.hidden_ref
  125.9 13.2 %all-to-all-done.2 = bf16[8,8,5120]{2,1,0:T(8,128)(2,1)} async-done(((bf16[8,8,5120]{2,1,0:T(8,128)(2,1)}), bf16[8,8,5120]{2,1,0:T(8,128)(2,1)}, u32[]{:S(2)}, u32[]{:S(2)}) %all-to-all-start.2) | async-done | bytes 655392 | tf_op jit(solution)/shard_map/all_to_all | solution.py:375
  139.1 2.2 %convolution_convert_fusion = bf16[64,5120]{1,0:T(8,128)(2,1)} fusion(bf16[8,8,5120]{2,1,0:T(8,128)(2,1)} %all-to-all-done.2, s32[64]{0:T(128)S(1)} %select_reduce_fusion), kind=kOutput, calls=%fused_computation.2 | convolution fusion | flops 42274816 | bytes 1310976 | tf_op jit(solution)/shard_map/dot_general | solution.py:383
  141.4 5.1 %reshape.130 = bf16[64,16,2,160]{3,2,1,0:T(2,128)(2,1)} reshape(bf16[64,5120]{1,0:T(8,128)(2,1)} %convolution_convert_fusion) | data formatting | bytes 1310720 | tf_op jit(solution)/shard_map/reshape | solution.py:384
  146.5 5.4 %convert_add_fusion = f32[1024,1280]{1,0:T(8,128)S(1)} fusion(bf16[1024,1280]{1,0:T(8,128)(2,1)} %collective-permute-done.3, bf16[1024,1024]{1,0:T(8,128)(2,1)S(1)} %copy-done.1, bf16[1024,1280]{1,0:T(8,128)(2,1)} %bitcast.53), kind=kOutput, calls=%fused_computation.5 | convolution fusion | flops 2686976000 | bytes 12582912 | tf_op jit(solution)/shard_map/dot_general | solution.py:339
  152.3 39.8 %shard_map.105 = bf16[1024,640]{1,0:T(8,128)(2,1)S(1)} custom-call(f32[4,8,32,640]{3,2,1,0:T(8,128)S(1)} %slice.47.kept_ref, bf16[1,4,8,32,640]{4,3,2,1,0:T(8,128)(2,1)S(1)} %fusion.8.leaving_ref, s32[4,1,256]{2,1,0:T(1,128)S(1)} %reshape.128.order_ref, bf16[1024,640]{1,0:T(8,128)(2,1)S(1)} %constant_dynamic-slice_fusion.1.hidden_ref), custom_call_target="tpu_custom_call" | custom-call | flops 1342177280 | bytes 16777216 | tf_op jit(solution)/shard_map/pallas_call | solution.py:233
  (75 shorter events, 11.5 us)
Async XLA Ops:
  0.7 3.6 %copy-start.11 = (s32[1,1024]{1,0:T(1,128)S(1)}, s32[1,1024]{1,0:T(1,128)}, u32[]{:S(2)}) copy-start(s32[1,1024]{1,0:T(1,128)} %param.11) | copy-start | bytes 12292
  0.7 3.7 %copy-start.14 = (bf16[2560]{0:T(1024)(128)(2,1)S(1)}, bf16[2560]{0:T(1024)(128)(2,1)}, u32[]{:S(2)}) copy-start(bf16[2560]{0:T(1024)(128)(2,1)} %param.13) | copy-start | bytes 15364
  7.9 2.2 %copy-start.4 = (bf16[1024,640]{1,0:T(8,128)(2,1)}, bf16[1024,640]{1,0:T(8,128)(2,1)S(1)}, u32[]{:S(2)}) copy-start(bf16[1024,640]{1,0:T(8,128)(2,1)S(1)} %get-tuple-element.13) | copy-start | bytes 3932164
  10.1 28.3 %all-to-all-start = ((bf16[8,80,640]{2,1,0:T(8,128)(2,1)}), bf16[8,80,640]{2,1,0:T(8,128)(2,1)}, u32[]{:S(2)}, u32[]{:S(2)}) async-start(bf16[8,80,640]{2,1,0:T(8,128)(2,1)} %bitcast.1), calls=%async_computation | async-start | bytes 1638400 | tf_op jit(solution)/shard_map/all_to_all | solution.py:306
  21.5 2.9 %copy-start.6 = (bf16[2560,160]{0,1:T(8,128)(2,1)S(1)}, bf16[2560,160]{0,1:T(8,128)(2,1)}, u32[]{:S(2)}) copy-start(bf16[2560,160]{0,1:T(8,128)(2,1)} %param.15) | copy-start | bytes 2457604
  24.4 1.1 copy-start.7
  24.4 1.3 copy-start.12
  26.3 2.4 %copy-start.3 = (bf16[1024,640]{1,0:T(8,128)(2,1)S(1)}, bf16[1024,640]{1,0:T(8,128)(2,1)}, u32[]{:S(2)}) copy-start(bf16[1024,640]{1,0:T(8,128)(2,1)} %get-tuple-element.12) | copy-start | bytes 3932164
  26.3 2.7 %copy-start.5 = (bf16[1024,640]{1,0:T(8,128)(2,1)S(1)}, bf16[1024,640]{1,0:T(8,128)(2,1)}, u32[]{:S(2)}) copy-start(bf16[1024,640]{1,0:T(8,128)(2,1)} %copy-done.4) | copy-start | bytes 3932164
  38.4 28.4 %all-to-all-start.1 = ((bf16[8,48,1280]{2,1,0:T(8,128)(2,1)}), bf16[8,48,1280]{2,1,0:T(8,128)(2,1)}, u32[]{:S(2)}, u32[]{:S(2)}) async-start(bf16[8,48,1280]{2,1,0:T(8,128)(2,1)} %bitcast.58), calls=%async_computation.1 | async-start | bytes 1966080 | tf_op jit(solution)/shard_map/all_to_all | solution.py:306
  44.3 19.2 %collective-permute-start = (bf16[640,640]{1,0:T(8,128)(2,1)}, bf16[640,640]{1,0:T(8,128)(2,1)S(1)}, u32[]{:S(2)}, u32[]{:S(2)}) collective-permute-start(bf16[640,640]{1,0:T(8,128)(2,1)} %bitcast.2), channel_id=1, source_target_pairs={{2,0},{3,1},{0,2},{1,3},{6,4},{7,5},{4,6},{5,7},{10,8},{11,9},{8,1... | collective-permute-start | bytes 2457608 | tf_op jit(solution)/shard_map/ppermute | solution.py:279
  52.0 14.0 %copy-start.13 = (s32[8,64]{1,0:T(8,128)S(1)}, s32[8,64]{1,0:T(8,128)}, u32[]{:S(2)}) copy-start(s32[8,64]{1,0:T(8,128)} %param.12) | copy-start | bytes 6148
  52.0 14.8 %copy-start.8 = (f32[1024,40]{0,1:T(8,128)S(1)}, f32[1024,40]{0,1:T(8,128)}, u32[]{:S(2)}) copy-start(f32[1024,40]{0,1:T(8,128)} %get-tuple-element.28) | copy-start | bytes 491524
  52.0 14.8 %copy-start.9 = (f32[1024,40]{0,1:T(8,128)S(1)}, f32[1024,40]{0,1:T(8,128)}, u32[]{:S(2)}) copy-start(f32[1024,40]{0,1:T(8,128)} %get-tuple-element.29) | copy-start | bytes 491524
  52.0 14.8 %copy-start.10 = (f32[1024,40]{0,1:T(8,128)S(1)}, f32[1024,40]{0,1:T(8,128)}, u32[]{:S(2)}) copy-start(f32[1024,40]{0,1:T(8,128)} %get-tuple-element.30) | copy-start | bytes 491524
  66.0 13.2 %collective-permute-start.1 = (bf16[640,1280]{1,0:T(8,128)(2,1)}, bf16[640,1280]{1,0:T(8,128)(2,1)}, u32[]{:S(2)}, u32[]{:S(2)}) collective-permute-start(bf16[640,1280]{1,0:T(8,128)(2,1)} %pad_maximum_fusion.7), channel_id=1, source_target_pairs={{1,0},{0,1},{3,2},{2,3},{5,4},{4,5},{7,6},{6,7},{9,8},{8,9},{11,10... | collective-permute-start | bytes 4915208 | tf_op jit(solution)/shard_map/ppermute | solution.py:283
  66.8 9.4 %collective-permute-start.2 = (bf16[384,1280]{1,0:T(8,128)(2,1)}, bf16[384,1280]{1,0:T(8,128)(2,1)}, u32[]{:S(2)}, u32[]{:S(2)}) collective-permute-start(bf16[384,1280]{1,0:T(8,128)(2,1)} %bitcast.10), channel_id=1, source_target_pairs={{1,0},{0,1},{3,2},{2,3},{5,4},{4,5},{7,6},{6,7},{9,8},{8,9},{11,10... | collective-permute-start | bytes 2949128 | tf_op jit(solution)/shard_map/ppermute | solution.py:283
  105.4 4.1 %copy-start = (bf16[1024,1024]{1,0:T(8,128)(2,1)}, bf16[1024,1024]{1,0:T(8,128)(2,1)S(1)}, u32[]{:S(2)}) copy-start(bf16[1024,1024]{1,0:T(8,128)(2,1)S(1)} %get-tuple-element.5) | copy-start | bytes 6291460
  109.6 37.0 %collective-permute-start.3 = (bf16[1024,1280]{1,0:T(8,128)(2,1)}, bf16[1024,1280]{1,0:T(8,128)(2,1)}, u32[]{:S(2)}, u32[]{:S(2)}) collective-permute-start(bf16[1024,1280]{1,0:T(8,128)(2,1)} %convolution_convert_fusion.2), channel_id=1, source_target_pairs={{1,0},{0,1},{3,2},{2,3},{5,4},{4,5},{7,6},{6,7},{9,8},{8,9},{11,10... | collective-permute-start | bytes 7864328 | tf_op jit(solution)/shard_map/ppermute | solution.py:283
  114.2 7.0 %copy-start.2 = (bf16[640,1280]{1,0:T(8,128)(2,1)S(1)}, bf16[640,1280]{1,0:T(8,128)(2,1)}, u32[]{:S(2)}) copy-start(bf16[640,1280]{1,0:T(8,128)(2,1)} %get-tuple-element.34) | copy-start | bytes 4915204
  116.0 23.1 %all-to-all-start.2 = ((bf16[8,8,5120]{2,1,0:T(8,128)(2,1)}), bf16[8,8,5120]{2,1,0:T(8,128)(2,1)}, u32[]{:S(2)}, u32[]{:S(2)}) async-start(bf16[8,8,5120]{2,1,0:T(8,128)(2,1)} %fusion), calls=%async_computation.2 | async-start | bytes 1310720 | tf_op jit(solution)/shard_map/all_to_all | solution.py:375
  124.3 22.2 %copy-start.1 = (bf16[1024,1024]{1,0:T(8,128)(2,1)S(1)}, bf16[1024,1024]{1,0:T(8,128)(2,1)}, u32[]{:S(2)}) copy-start(bf16[1024,1024]{1,0:T(8,128)(2,1)} %copy-done) | copy-start | bytes 6291460

commit v2 on v1

--- a/solution.py
+++ b/solution.py
@@ -135,8 +135,8 @@
 
 
 def return_kernel(
-    axes, kept_ref, leaving_ref, order_ref, hidden_ref, out_ref,
-    crossed, fin, ret, total, x_send, x_recv, r_send, r_recv,
+    axes, kept_ref, leaving_ref, order_ref, hidden_ref, page_ref, place_ref, out_ref, cache_ref,
+    pages, p_send, p_recv, crossed, fin, ret, total, x_send, x_recv, r_send, r_recv,
 ):
     groups, xs, cores = axes
     steps, _, run, part = kept_ref.shape
@@ -183,9 +183,30 @@
             device_id=(group(k), tp), device_id_type=mesh_ids,
         )
 
+    def page_copy(k):
+        return pltpu.make_async_remote_copy(
+            src_ref=page_ref.at[group(k)], dst_ref=pages.at[me],
+            send_sem=p_send.at[k], recv_sem=p_recv.at[k],
+            device_id=(group(k), tp), device_id_type=mesh_ids,
+        )
+
+    def page_arrival(k):
+        source = group(groups - k)
+        return pltpu.make_async_remote_copy(
+            src_ref=page_ref.at[source], dst_ref=pages.at[source],
+            send_sem=p_send.at[k], recv_sem=p_recv.at[k],
+            device_id=(group(k), tp), device_id_type=mesh_ids,
+        )
+
     for step in range(steps):
         for k in range(1, xs):
             x_copy(step, k).start()
+
+    @pl.loop(1, groups)
+    def _(k):
+        page_copy(k).start()
+
+    pages[me] = page_ref[me]
     total[...] = hidden_ref[...].astype(F32)
 
     def take(step):
@@ -212,8 +233,21 @@
         ret[step, me] = fin[step, me]
         if step > 0:
             take(step - 1)
+
+    @pl.loop(1, groups)
+    def _(k):
+        page_arrival(k).wait_recv()
+
+    row = lax.broadcasted_iota(jnp.int32, (length, length), 0)
+    place = (row == place_ref[...]).astype(F32).astype(BF16)
+    rows = pages[...].reshape(length, pages.shape[-1])
+    cache_ref[...] = jnp.dot(place, rows, preferred_element_type=F32).astype(BF16)
     take(steps - 1)
     out_ref[...] = total[...].astype(BF16)
+
+    @pl.loop(1, groups)
+    def _(k):
+        page_copy(k).wait_send()
 
     for step in range(steps):
         for k in range(1, xs):
@@ -224,7 +258,7 @@
             ret_copy(step, k).wait_send()
 
 
-def give_back(axes, kept, leaving, order, hidden_own):
+def give_back(axes, kept, leaving, order, hidden_own, page_rows, place):
     groups, xs, _ = axes
     steps, _, run, part = kept.shape
     length = hidden_own.shape[0]
@@ -232,10 +266,14 @@
     dma = pltpu.SemaphoreType.DMA
     return pl.pallas_call(
         functools.partial(return_kernel, axes),
-        out_shape=jax.ShapeDtypeStruct((length, part), BF16),
-        in_specs=[vmem] * 4,
-        out_specs=vmem,
+        out_shape=[
+            jax.ShapeDtypeStruct((length, part), BF16),
+            jax.ShapeDtypeStruct((length, page_rows.shape[-1]), BF16),
+        ],
+        in_specs=[vmem] * 6,
+        out_specs=[vmem] * 2,
         scratch_shapes=[
+            pltpu.VMEM(page_rows.shape, BF16), dma((groups,)), dma((groups,)),
             pltpu.VMEM((xs - 1, steps, groups, run, part), BF16),
             pltpu.VMEM((steps, groups, run, part), BF16),
             pltpu.VMEM((steps, groups, run, part), BF16),
@@ -249,7 +287,7 @@
         cost_estimate=pl.CostEstimate(
             flops=2 * length * length * part, bytes_accessed=16 * 2**20, transcendentals=0
         ),
-    )(kept, leaving, order, hidden_own)
+    )(kept, leaving, order, hidden_own, page_rows, place)
 
 
 def one_hot_rows(index, count):
@@ -343,12 +381,6 @@
     kept = kept.reshape(steps, groups, run, -1)
     leaving = [kept[..., k * part : (k + 1) * part].astype(BF16) for k in range(1, xs)]
     order_steps = order_grid.reshape(groups, steps, run).transpose(1, 0, 2)
-    hidden_out = give_back(
-        (groups, xs, cores), kept[..., :part], jnp.stack(leaving),
-        order_steps.reshape(steps, 1, groups * run),
-        lax.dynamic_slice_in_dim(hidden, tp_place * part, part, 1),
-    )
-
     pages_dev = length // PAGE
     per_owner = pages_dev // groups
     my_req = lax.axis_index("req")
@@ -367,20 +399,27 @@
             value_pad[:, at : at + HD],
         ]
     kv_rows = jnp.concatenate(columns, axis=1)
-    page_rows = kv_rows.reshape(pages_dev, PAGE * kv_local * 2 * HD)
+    tokens = jnp.arange(PAGE, dtype=jnp.int32)[None, :]
+    row_slots = (my_slots[:, None] * PAGE + tokens).reshape(-1)
+    row_numbers = jnp.arange(length, dtype=jnp.int32)
     page_rows = jnp.dot(
-        (my_slots[None, :] == numbers[:, None]).astype(BF16), page_rows,
+        (row_slots[None, :] == row_numbers[:, None]).astype(BF16), kv_rows,
         preferred_element_type=F32,
-    ).astype(BF16)
-    arrived = lax.all_to_all(page_rows, "req", split_axis=0, concat_axis=0, tiled=True)
+    ).astype(BF16).reshape(groups, share, -1)
     slot_here = jnp.where(
         owners == my_req, jnp.arange(groups, dtype=jnp.int32)[:, None] * per_owner + rank, -1
     ).reshape(-1)
     target = (page_table % pages_dev).reshape(-1)
     hit = (slot_here[:, None] == numbers[None, :]).astype(jnp.int32)
     slot_target = jnp.sum(hit * target[:, None], axis=0)
-    place = (slot_target[None, :] == numbers[:, None]).astype(BF16)
-    kv_cache = jnp.dot(place, arrived, preferred_element_type=F32).astype(BF16)
+    place = (slot_target[:, None] * PAGE + tokens).reshape(1, -1)
+
+    hidden_out, kv_cache = give_back(
+        (groups, xs, cores), kept[..., :part], jnp.stack(leaving),
+        order_steps.reshape(steps, 1, groups * run),
+        lax.dynamic_slice_in_dim(hidden, tp_place * part, part, 1),
+        page_rows, place,
+    )
     return (hidden_out, kv_cache.reshape(pages_dev, PAGE, kv_local, 2 * HD))
 
 

time: 194 us -> 186 us (0.959)
  waiting for transfers between devices: 30.6 us -> 17.3 us
  Pallas kernels: 57.9 us -> 67.9 us
  starting transfers between devices: 18.7 us -> 13.8 us
    all_to_all x1 -> x0, waiting for transfers between devices: 13.2 us -> none  [local(): lax.all_to_all(page_rows, 'req', split_axis=0, concat_axis=0, tiled=True)]
    pallas_call x1, Pallas kernels: 39.8 us -> 49.9 us  [give_back(): pl.pallas_call(functools.partial(return_kernel, axes), out_shape=[jax.Sha...]
    all_to_all x1 -> x0, starting transfers between devices: 5.04 us -> none  [local(): lax.all_to_all(page_rows, 'req', split_axis=0, concat_axis=0, tiled=True)]
    unnamed x33 -> x29, local copies, waits for them, and re-layouts: 7.02 us -> 8.79 us
  transfers between devices with their start and end apart: 7 -> 6, of which waited for: 4 -> 3; matrix products, arithmetic and copies ran while one was open for 28% -> 26% of each run, Pallas kernels for 0% -> 0%
where the time goes in v2:
time: 186 us; the launch traced here: 185 us
  Pallas kernels  67.9 us (37%)
  local copies, waits for them, and re-layouts  34.1 us (18%)
  matrix products  30.8 us (17%)
  other arithmetic  20.4 us (11%)
  waiting for transfers between devices  17.3 us (9%)
  starting transfers between devices  13.8 us (7%)
    pallas_call x1, Pallas kernels, give_back(): pl.pallas_call(functools.partial(return_kernel, axes), out_shape=[jax.Sha...  49.9 us
    pallas_call x1, Pallas kernels, attention(): pl.pallas_call(functools.partial(attention_kernel, cuts, groups, heads, k...  18.1 us
    all_to_all x2, starting transfers between devices, deal(): return lax.all_to_all(sent, 'req', split_axis=0, concat_axis=0, tiled=True)  11.7 us
    ppermute x1, waiting for transfers between devices, from_x(): return lax.ppermute(array, 'tp', pairs)  11.5 us
    unnamed x29, local copies, waits for them, and re-layouts  8.79 us
    dot_general x2, matrix products, local(): raw = raw + jnp.dot(other, weights[half:], preferred_element_type=F32)  7.15 us
    dot_general x2, matrix products, local(): raw = jnp.dot(mine, weights[:half], preferred_element_type=F32)  6.79 us
    concatenate x1, other arithmetic, local(): jnp.concatenate([padded_halves(w_query), padded_halves(w_key), padded_hea...  6.22 us
  transfers between devices with their start and end apart: 6, of which 3 were waited for; matrix products, arithmetic and copies ran while one was open for 26% of the time, Pallas kernels for 0%

profile of v2, /device:TPU:0, one launch (start us, length us, event | category | flops | bytes accessed | tf_op | source)
XLA Modules:
  0.0 185.5 jit_solution(11356646776475730490)
XLA Ops:
  0.7 3.6 %multiply_reduce_fusion = f32[1024]{0:T(1024)S(1)} fusion(bf16[1024,2560]{1,0:T(8,128)(2,1)} %param.9), kind=kLoop, calls=%fused_computation | loop fusion | flops 7863296 | bytes 5246976 | tf_op jit(solution)/shard_map/reduce_sum | solution.py:327
  4.5 3.5 %multiply_convert_fusion = (bf16[1024,640]{1,0:T(8,128)(2,1)}, bf16[1024,640]{1,0:T(8,128)(2,1)S(1)}) fusion(f32[640]{0:T(1024)S(1)} %get-tuple-element.30, bf16[1024,2560]{1,0:T(8,128)(2,1)} %param.9, s32[]{:T(128)S(6)} %select_n.55, f32[1024]{0:T(1024)S(1)} %add_rsqrt_fusion, f32[640]{0:T(1024)S(1)} %get-tuple-element.31, s32[]{:T(128)S(6)} %select_n.54), kind=kLoop, calls=%fused_computation.16 | loop fusion | flops 5242880 | bytes 5252104 | tf_op jit(solution)/shard_map/convert_element_type | solution.py:332
  7.9 2.2 %fusion.8 = bf16[640,640]{1,0:T(8,128)(2,1)} fusion(bf16[1024,640]{1,0:T(8,128)(2,1)S(1)} %get-tuple-element.17, s32[640]{0:T(1024)S(1)} %eq.81), kind=kOutput, calls=%fused_computation.27 | convolution fusion | flops 839925760 | bytes 2132480 | tf_op jit(solution)/shard_map/dot_general | solution.py:340
  10.1 7.3 %all-to-all-start = ((bf16[8,80,640]{2,1,0:T(8,128)(2,1)}), bf16[8,80,640]{2,1,0:T(8,128)(2,1)}, u32[]{:S(2)}, u32[]{:S(2)}) async-start(bf16[8,80,640]{2,1,0:T(8,128)(2,1)} %bitcast.1), calls=%async_computation | async-start | bytes 1638400 | tf_op jit(solution)/shard_map/all_to_all | solution.py:344
  17.5 4.0 %copy.21 = bf16[2560,640]{0,1:T(8,128)(2,1)S(1)} copy(bf16[2560,640]{1,0:T(8,128)(2,1)} %param.14) | data formatting | bytes 6553600 | tf_op args[5]
  21.5 2.9 %pad.26 = bf16[2560,8,2,64]{0,3,2,1:T(8,128)(2,1)} pad(bf16[2560,8,2,40]{0,3,2,1:T(8,128)(2,1)S(1)} %bitcast.42, bf16[]{:T(256)} %constant.82.clone.1), padding=0_0x0_0x0_0x0_24 | pad | bytes 8519682 | tf_op jit(solution)/shard_map/jit(_pad)/pad | solution.py:27
  24.5 1.0 copy-done.6
  26.4 2.3 %constant_dynamic-slice_fusion.3 = (bf16[640,640]{1,0:T(8,128)(2,1)S(1)}, bf16[640,640]{1,0:T(8,128)(2,1)S(1)}, bf16[640,640]{1,0:T(8,128)(2,1)S(1)}, bf16[640,640]{1,0:T(8,128)(2,1)S(1)}) fusion(bf16[640,2560]{1,0:T(8,128)(2,1)} %param.17, s32[]{:T(128)S(6)} %select_n.56, s32[]{:T(128)S(6)} %select_n.55, s32[]{:T(128)S(6)} %select_n.54, s32[]{:T(128)S(6)} %select_n.57), kind=kLoop, calls=%fused_computation.58 | loop fusion | bytes 6553616 | tf_op jit(solution)/shard_map/dynamic_slice | solution.py:352
  29.1 2.2 %convolution_convert_fusion.1 = bf16[384,1280]{1,0:T(8,128)(2,1)} fusion(bf16[1024,640]{1,0:T(8,128)(2,1)S(1)} %copy-done.2, bf16[1024,640]{1,0:T(8,128)(2,1)S(1)} %copy-done.4, s32[384]{0:T(512)S(1)} %eq.85), kind=kOutput, calls=%fused_computation.11 | convolution fusion | flops 1012760576 | bytes 3606016 | tf_op jit(solution)/shard_map/dot_general | solution.py:340
  31.3 1.9 %pad_maximum_fusion.8 = (bf16[640,1280]{1,0:T(8,128)(2,1)}, bf16[640,1280]{1,0:T(8,128)(2,1)}) fusion(bf16[640,640]{1,0:T(8,128)(2,1)S(1)} %get-tuple-element.19, bf16[640,640]{1,0:T(8,128)(2,1)S(1)} %get-tuple-element.20, bf16[640,640]{1,0:T(8,128)(2,1)S(1)} %get-tuple-element.21, bf16[640,640]{1,0:T(8,128)(2,1)S(1)} %get-tuple-element.18), kind=kLoop, calls=%fused_computation.24 | loop fusion | flops 6553600 | bytes 6553600 | tf_op jit(solution)/shard_map/concatenate | solution.py:353
  33.2 5.2 %all-to-all-done = bf16[8,80,640]{2,1,0:T(8,128)(2,1)} async-done(((bf16[8,80,640]{2,1,0:T(8,128)(2,1)}), bf16[8,80,640]{2,1,0:T(8,128)(2,1)}, u32[]{:S(2)}, u32[]{:S(2)}) %all-to-all-start) | async-done | bytes 819232 | tf_op jit(solution)/shard_map/all_to_all | solution.py:344
  38.4 4.4 %all-to-all-start.1 = ((bf16[8,48,1280]{2,1,0:T(8,128)(2,1)}), bf16[8,48,1280]{2,1,0:T(8,128)(2,1)}, u32[]{:S(2)}, u32[]{:S(2)}) async-start(bf16[8,48,1280]{2,1,0:T(8,128)(2,1)} %bitcast.55), calls=%async_computation.1 | async-start | bytes 1966080 | tf_op jit(solution)/shard_map/all_to_all | solution.py:344
  42.9 1.6 collective-permute-start
  44.5 6.2 %pad_maximum_fusion = bf16[2560,1536]{0,1:T(8,128)(2,1)} fusion(bf16[2560,256]{0,1:T(8,128)(2,1)S(1)} %bitcast.46, bf16[2560,256]{0,1:T(8,128)(2,1)S(1)} %bitcast.45, bf16[2560,1024]{0,1:T(8,128)(2,1)} %bitcast.41), kind=kLoop, calls=%fused_computation.1 | loop fusion | flops 23592960 | bytes 15728640 | tf_op jit(solution)/shard_map/concatenate | solution.py:346
  50.7 11.5 %collective-permute-done = bf16[640,640]{1,0:T(8,128)(2,1)S(1)} collective-permute-done((bf16[640,640]{1,0:T(8,128)(2,1)}, bf16[640,640]{1,0:T(8,128)(2,1)S(1)}, u32[]{:S(2)}, u32[]{:S(2)}) %collective-permute-start) | collective-permute-done | bytes 819232 | tf_op jit(solution)/shard_map/ppermute | solution.py:317
  63.0 2.5 %pad_maximum_fusion.7 = bf16[640,1280]{1,0:T(8,128)(2,1)} fusion(bf16[640,640]{1,0:T(8,128)(2,1)S(1)} %collective-permute-done, bf16[640,640]{1,0:T(8,128)(2,1)} %bitcast.2), kind=kLoop, calls=%fused_computation.23 | loop fusion | flops 3276800 | bytes 3276800 | tf_op jit(solution)/shard_map/concatenate | solution.py:360
  67.6 1.6 pad.32
  69.3 4.0 %constant_dynamic-slice_fusion.9 = (bf16[640,1536]{0,1:T(8,128)(2,1)S(1)}, bf16[640,1536]{0,1:T(8,128)(2,1)S(1)}, bf16[640,1536]{0,1:T(8,128)(2,1)S(1)}, bf16[640,1536]{0,1:T(8,128)(2,1)S(1)}) fusion(bf16[2560,1536]{0,1:T(8,128)(2,1)} %pad_maximum_fusion, s32[]{:T(128)S(6)} %select_n.54, s32[]{:T(128)S(6)} %select_n.57, s32[]{:T(128)S(6)} %select_n.56, ...), kind=kLoop, calls=%fused_computation.64 | loop fusion | bytes 15728656 | tf_op jit(solution)/shard_map/dynamic_slice | solution.py:350
  73.3 2.9 %fusion.6 = f32[384,1536]{1,0:T(8,128)S(1)} fusion(bf16[384,1280]{1,0:T(8,128)(2,1)} %bitcast.10, bf16[640,1536]{0,1:T(8,128)(2,1)S(1)} %get-tuple-element.15, bf16[640,1536]{0,1:T(8,128)(2,1)S(1)} %get-tuple-element.12), kind=kOutput, calls=%fused_computation.21 | convolution fusion | flops 1517813760 | bytes 7274496 | tf_op jit(solution)/shard_map/dot_general | solution.py:364
  76.2 2.9 %convolution_add_fusion.1.refs_1_ = f32[384,1536]{1,0:T(8,128)S(1)} fusion(f32[384,1536]{1,0:T(8,128)S(1)} %fusion.6, bf16[384,1280]{1,0:T(8,128)(2,1)} %collective-permute-done.2, bf16[640,1536]{0,1:T(8,128)(2,1)S(1)} %get-tuple-element.13, bf16[640,1536]{0,1:T(8,128)(2,1)S(1)} %get-tuple-element.14), kind=kOutput, calls=%fused_computation.10 | convolution fusion | flops 1518403584 | bytes 9633792 | tf_op jit(solution)/shard_map/dot_general | solution.py:367
  79.2 4.2 %fusion.5 = f32[640,1536]{1,0:T(8,128)S(1)} fusion(bf16[640,1280]{1,0:T(8,128)(2,1)} %collective-permute-done.1, bf16[640,1536]{0,1:T(8,128)(2,1)S(1)} %get-tuple-element.13, bf16[640,1536]{0,1:T(8,128)(2,1)S(1)} %get-tuple-element.14), kind=kOutput, calls=%fused_computation.20 | convolution fusion | flops 2524446720 | bytes 9502720 | tf_op jit(solution)/shard_map/dot_general | solution.py:367
  83.4 3.9 %convolution_add_fusion.refs_0_ = f32[640,1536]{1,0:T(8,128)S(1)} fusion(f32[640,1536]{1,0:T(8,128)S(1)} %fusion.5, bf16[640,1536]{0,1:T(8,128)(2,1)S(1)} %get-tuple-element.15, bf16[640,1536]{0,1:T(8,128)(2,1)S(1)} %get-tuple-element.12, bf16[640,640]{1,0:T(8,128)(2,1)S(1)} %copy-done.8, bf16[640,640]{1,0:T(8,128)(2,1)} %bitcast.2), kind=kOutput, calls=%fused_computation.9 | convolution fusion | flops 2528706560 | bytes 13434880 | tf_op jit(solution)/shard_map/dot_general | solution.py:364
  87.3 18.1 %shard_map.104 = (bf16[1024,1024]{1,0:T(8,128)(2,1)S(1)}, bf16[1024,256]{1,0:T(8,128)(2,1)S(1)}, bf16[1024,256]{1,0:T(8,128)(2,1)S(1)}) custom-call(f32[640,1536]{1,0:T(8,128)S(1)} %convolution_add_fusion.refs_0_, f32[384,1536]{1,0:T(8,128)S(1)} %convolution_add_fusion.1.refs_1_, f32[1024,128]{1,0:T(8,128)S(1)} %copy.22.refs_2_, ...), custom_call_target="tpu_custom_call" | custom-call | flops 2684354560 | bytes 10485760 | tf_op jit(solution)/shard_map/pallas_call | solution.py:119
  105.4 4.2 %convolution_convert_fusion = bf16[1024,1280]{1,0:T(8,128)(2,1)} fusion(bf16[1024,1024]{1,0:T(8,128)(2,1)S(1)} %get-tuple-element.7, bf16[1024,1280]{1,0:T(8,128)(2,1)S(1)} %bitcast.50), kind=kOutput, calls=%fused_computation.8 | convolution fusion | flops 2685665280 | bytes 7340032 | tf_op jit(solution)/shard_map/dot_general | solution.py:379
  110.7 3.2 %pad.31 = bf16[8,128,1280]{2,1,0:T(8,128)(2,1)} pad(bf16[8,80,1280]{2,1,0:T(8,128)(2,1)} %bitcast.43, bf16[]{:T(256)} %constant.82.clone.1), padding=0_0x0_48x0_0 | pad | bytes 4259842 | tf_op jit(solution)/shard_map/jit(_pad)/pad | solution.py:35
  115.6 1.4 constant_dynamic-slice_fusion.1.hidden_ref
  117.4 3.3 %concatenate.40 = bf16[1024,320]{1,0:T(8,128)(2,1)} concatenate(bf16[1024,40]{1,0:T(8,128)(2,1)S(1)} %get-tuple-element.27, bf16[1024,40]{1,0:T(8,128)(2,1)S(1)} %get-tuple-element.26, bf16[1024,80]{1,0:T(8,128)(2,1)S(1)} %get-tuple-element.23, bf16[1024,40]{1,0:T(8,128)(2,1)S(1)} %get-tuple-element.25, bf16[1024,40]{1,0:T(8,128)(2,1)S(1)} %get-tuple-element.24, ...), dimensions={1} | concatenate | bytes 1310720 | tf_op jit(solution)/shard_map/concatenate | solution.py:401
  120.7 2.2 %fusion.9 = bf16[1024,320]{0,1:T(8,128)(2,1)S(1)} fusion(bf16[1024,320]{1,0:T(8,128)(2,1)} %concatenate.40, s32[1024]{0:T(1024)S(1)} %add.163), kind=kOutput, calls=%fused_computation.28 | convolution fusion | flops 672464896 | bytes 1314816 | tf_op jit(solution)/shard_map/dot_general | solution.py:405
  123.3 6.0 %convert_add_fusion = f32[1024,1280]{1,0:T(8,128)S(1)} fusion(bf16[1024,1280]{1,0:T(8,128)(2,1)} %collective-permute-done.3, bf16[1024,1024]{1,0:T(8,128)(2,1)} %copy-done.1, bf16[1024,1280]{1,0:T(8,128)(2,1)} %bitcast.49), kind=kOutput, calls=%fused_computation.2 | convolution fusion | flops 2686976000 | bytes 12582912 | tf_op jit(solution)/shard_map/dot_general | solution.py:377
  129.8 49.9 %shard_map.105 = (bf16[1024,640]{1,0:T(8,128)(2,1)S(1)}, bf16[1024,320]{1,0:T(8,128)(2,1)S(1)}) custom-call(f32[4,8,32,640]{3,2,1,0:T(8,128)S(1)} %slice.47.kept_ref, bf16[1,4,8,32,640]{4,3,2,1,0:T(8,128)(2,1)S(1)} %fusion.10.leaving_ref, s32[4,1,256]{2,1,0:T(1,128)S(1)} %reshape.175.order_ref, ...), custom_call_target="tpu_custom_call" | custom-call | flops 1342177280 | bytes 16777216 | tf_op jit(solution)/shard_map/pallas_call | solution.py:267
  180.5 3.9 %reshape.177 = bf16[64,16,2,160]{3,2,1,0:T(2,128)(2,1)} reshape(bf16[1024,320]{1,0:T(8,128)(2,1)} %copy-done) | data formatting | bytes 1310720 | tf_op jit(solution)/shard_map/reshape | solution.py:423
  184.4 1.1 copy.30
  (73 shorter events, 9.2 us)
Async XLA Ops:
  0.7 3.6 %copy-start.9 = (s32[1,1024]{1,0:T(1,128)S(1)}, s32[1,1024]{1,0:T(1,128)}, u32[]{:S(2)}) copy-start(s32[1,1024]{1,0:T(1,128)} %param.11) | copy-start | bytes 12292
  0.7 3.7 %copy-start.12 = (bf16[2560]{0:T(1024)(128)(2,1)S(1)}, bf16[2560]{0:T(1024)(128)(2,1)}, u32[]{:S(2)}) copy-start(bf16[2560]{0:T(1024)(128)(2,1)} %param.13) | copy-start | bytes 15364
  7.9 2.2 %copy-start.3 = (bf16[1024,640]{1,0:T(8,128)(2,1)}, bf16[1024,640]{1,0:T(8,128)(2,1)S(1)}, u32[]{:S(2)}) copy-start(bf16[1024,640]{1,0:T(8,128)(2,1)S(1)} %get-tuple-element.17) | copy-start | bytes 3932164
  10.1 28.3 %all-to-all-start = ((bf16[8,80,640]{2,1,0:T(8,128)(2,1)}), bf16[8,80,640]{2,1,0:T(8,128)(2,1)}, u32[]{:S(2)}, u32[]{:S(2)}) async-start(bf16[8,80,640]{2,1,0:T(8,128)(2,1)} %bitcast.1), calls=%async_computation | async-start | bytes 1638400 | tf_op jit(solution)/shard_map/all_to_all | solution.py:344
  21.5 2.9 %copy-start.5 = (bf16[2560,160]{0,1:T(8,128)(2,1)S(1)}, bf16[2560,160]{0,1:T(8,128)(2,1)}, u32[]{:S(2)}) copy-start(bf16[2560,160]{0,1:T(8,128)(2,1)} %param.15) | copy-start | bytes 2457604
  24.4 1.1 copy-start.6
  24.4 1.3 copy-start.10
  26.3 2.4 %copy-start.2 = (bf16[1024,640]{1,0:T(8,128)(2,1)S(1)}, bf16[1024,640]{1,0:T(8,128)(2,1)}, u32[]{:S(2)}) copy-start(bf16[1024,640]{1,0:T(8,128)(2,1)} %get-tuple-element.16) | copy-start | bytes 3932164
  26.4 2.7 %copy-start.4 = (bf16[1024,640]{1,0:T(8,128)(2,1)S(1)}, bf16[1024,640]{1,0:T(8,128)(2,1)}, u32[]{:S(2)}) copy-start(bf16[1024,640]{1,0:T(8,128)(2,1)} %copy-done.3) | copy-start | bytes 3932164
  38.4 28.4 %all-to-all-start.1 = ((bf16[8,48,1280]{2,1,0:T(8,128)(2,1)}), bf16[8,48,1280]{2,1,0:T(8,128)(2,1)}, u32[]{:S(2)}, u32[]{:S(2)}) async-start(bf16[8,48,1280]{2,1,0:T(8,128)(2,1)} %bitcast.55), calls=%async_computation.1 | async-start | bytes 1966080 | tf_op jit(solution)/shard_map/all_to_all | solution.py:344
  42.9 19.2 %collective-permute-start = (bf16[640,640]{1,0:T(8,128)(2,1)}, bf16[640,640]{1,0:T(8,128)(2,1)S(1)}, u32[]{:S(2)}, u32[]{:S(2)}) collective-permute-start(bf16[640,640]{1,0:T(8,128)(2,1)} %bitcast.2), channel_id=1, source_target_pairs={{2,0},{3,1},{0,2},{1,3},{6,4},{7,5},{4,6},{5,7},{10,8},{11,9},{8,1... | collective-permute-start | bytes 2457608 | tf_op jit(solution)/shard_map/ppermute | solution.py:317
  62.1 0.9 copy-start.7
  65.6 13.6 %collective-permute-start.1 = (bf16[640,1280]{1,0:T(8,128)(2,1)}, bf16[640,1280]{1,0:T(8,128)(2,1)}, u32[]{:S(2)}, u32[]{:S(2)}) collective-permute-start(bf16[640,1280]{1,0:T(8,128)(2,1)} %pad_maximum_fusion.7), channel_id=1, source_target_pairs={{1,0},{0,1},{3,2},{2,3},{5,4},{4,5},{7,6},{6,7},{9,8},{8,9},{11,10... | collective-permute-start | bytes 4915208 | tf_op jit(solution)/shard_map/ppermute | solution.py:321
  66.8 9.4 %collective-permute-start.2 = (bf16[384,1280]{1,0:T(8,128)(2,1)}, bf16[384,1280]{1,0:T(8,128)(2,1)}, u32[]{:S(2)}, u32[]{:S(2)}) collective-permute-start(bf16[384,1280]{1,0:T(8,128)(2,1)} %bitcast.10), channel_id=1, source_target_pairs={{1,0},{0,1},{3,2},{2,3},{5,4},{4,5},{7,6},{6,7},{9,8},{8,9},{11,10... | collective-permute-start | bytes 2949128 | tf_op jit(solution)/shard_map/ppermute | solution.py:321
  79.2 4.3 %copy-start.8 = (bf16[640,640]{1,0:T(8,128)(2,1)S(1)}, bf16[640,640]{1,0:T(8,128)(2,1)}, u32[]{:S(2)}) copy-start(bf16[640,640]{1,0:T(8,128)(2,1)} %copy-done.7) | copy-start | bytes 2457604
  105.4 4.2 %copy-start.1 = (bf16[1024,1024]{1,0:T(8,128)(2,1)}, bf16[1024,1024]{1,0:T(8,128)(2,1)S(1)}, u32[]{:S(2)}) copy-start(bf16[1024,1024]{1,0:T(8,128)(2,1)S(1)} %get-tuple-element.7) | copy-start | bytes 6291460
  105.4 4.7 %copy-start.11 = (s32[8,64]{1,0:T(8,128)S(1)}, s32[8,64]{1,0:T(8,128)}, u32[]{:S(2)}) copy-start(s32[8,64]{1,0:T(8,128)} %param.12) | copy-start | bytes 6148
  109.6 13.7 %collective-permute-start.3 = (bf16[1024,1280]{1,0:T(8,128)(2,1)}, bf16[1024,1280]{1,0:T(8,128)(2,1)}, u32[]{:S(2)}, u32[]{:S(2)}) collective-permute-start(bf16[1024,1280]{1,0:T(8,128)(2,1)} %convolution_convert_fusion), channel_id=1, source_target_pairs={{1,0},{0,1},{3,2},{2,3},{5,4},{4,5},{7,6},{6,7},{9,8},{8,9},{11,10... | collective-permute-start | bytes 7864328 | tf_op jit(solution)/shard_map/ppermute | solution.py:321
  179.6 0.9 copy-start
